TPU v7x, 32 devices: a whole 2x2x4 slice. The times are simulated.
32 devices in a mesh: img: 8 (over z, x), band: 4 (over y, core).
Axes of the slice: x: 2, y: 2, z: 4, core: 2. Of those that a mesh axis runs over, the one named last changes fastest.
Arguments:
- image: bfloat16 [32, 16, 14, 256], P('img', 'band'), may hold values from -6 to 6
- conv_weight: bfloat16 [2304, 256], replicated, may hold values from -0.125 to 0.125
- gn_gain: float32 [256], replicated, may hold values from 0.5 to 1.5
- gn_bias: float32 [256], replicated, may hold values from -3 to 3
- embed_weight: bfloat16 [256, 768], replicated, may hold values from -0.5 to 0.5
- embed_bias: float32 [768], replicated, may hold values from -2 to 2
- ln1_gain: float32 [768], replicated, may hold values from 0.5 to 1.5
- ln1_bias: float32 [768], replicated, may hold values from -2 to 2
- qkv_weight: bfloat16 [768, 2304], replicated, may hold values from -0.21875 to 0.21875
- query_bias: float32 [768], replicated, may hold values from -2 to 2
- value_bias: float32 [768], replicated, may hold values from -2 to 2
- out_weight: bfloat16 [768, 768], replicated, may hold values from -0.875 to 0.875
- out_bias: float32 [768], replicated, may hold values from -2 to 2
- ln2_gain: float32 [768], replicated, may hold values from 0.5 to 1.5
- ln2_bias: float32 [768], replicated, may hold values from -2 to 2
- up_weight: bfloat16 [768, 3072], replicated, may hold values from -0.21875 to 0.21875
- up_bias: float32 [3072], replicated, may hold values from -3 to 3
- down_weight: bfloat16 [3072, 768], replicated, may hold values from -0.21875 to 0.21875
- down_bias: float32 [768], replicated, may hold values from -2 to 2
- text_embed: bfloat16 [32, 32, 768], P(('img', 'band')), may hold values from -6 to 6
- text_len: int32 [32], P(('img', 'band')), may hold values from 1 to 32, 640 in all
- cotangent: bfloat16 [32, 228, 768], P(('img', 'band')), may hold values from -14 to 14
Outputs:
- encoded: bfloat16 [32, 228, 768], P(('img', 'band'))
- image_grad: float32 [32, 16, 14, 256], P('img', 'band')
- text_grad: float32 [32, 32, 768], P(('img', 'band'))
- grad_conv_weight: float32 [2304, 256], P('img', 'band')
- grad_gn_gain: float32 [256], P('img')
- grad_gn_bias: float32 [256], P('img')
- grad_embed_weight: float32 [256, 768], P('img', 'band')
- grad_embed_bias: float32 [768], P('img')
- grad_ln1_gain: float32 [768], P('img')
- grad_ln1_bias: float32 [768], P('img')
- grad_qkv_weight: float32 [768, 2304], P('img', 'band')
- grad_query_bias: float32 [768], P('img')
- grad_value_bias: float32 [768], P('img')
- grad_out_weight: float32 [768, 768], P('band', 'img')
- grad_out_bias: float32 [768], P('img')
- grad_ln2_gain: float32 [768], P('img')
- grad_ln2_bias: float32 [768], P('img')
- grad_up_weight: float32 [768, 3072], P('img', 'band')
- grad_up_bias: float32 [3072], P('img')
- grad_down_weight: float32 [3072, 768], P('band', 'img')
- grad_down_bias: float32 [768], P('img')
Inputs may be any that keep to these rules, and one draw needn't show every extreme that they name: `text_len`: live text slots of each example; the largest is 32 in every draw.
All inputs are finite; a program needn't handle non-finite values. No bound on the sum of `text_len` on one device may be relied on, other than what follows from the above.
Results may differ from a plain program's by a relative error of at most 0.013.
Values may be sent and summed in bfloat16 or wider, within the bound.
A program may use at most 128 MiB of HBM per device.

v0:
```python
import jax
import jax.numpy as jnp
from jax import lax
from jax.sharding import PartitionSpec as P

D = 768
HEADS = 12
HD = 64
GROUPS = 32
GRID = 14
TEXT = 32
PATCHES = 196


def padded(cells, sides, width):
    for axis, dim in sides:
        count = lax.axis_size(axis)
        ends = count - 1
        head = lax.slice_in_dim(cells, 0, width, axis=dim)
        tail = lax.slice_in_dim(cells, cells.shape[dim] - width, cells.shape[dim], axis=dim)
        cells = jnp.concatenate(
            [
                lax.ppermute(tail, axis, [(i, (i + 1) % count) for i in range(ends)]),
                cells,
                lax.ppermute(head, axis, [((i + 1) % count, i) for i in range(ends)]),
            ],
            axis=dim,
        )
    return cells


def matmul(left, right):
    return jnp.dot(left, right, preferred_element_type=jnp.float32)


def norm_forward(values, gain, shift):
    mean = jnp.mean(values, -1, keepdims=True)
    cent = values - mean
    rstd = lax.rsqrt(jnp.mean(cent * cent, -1, keepdims=True) + 1e-06)
    normed = cent * rstd
    return (normed * gain + shift, normed, rstd)


def norm_backward(grad, normed, rstd, gain):
    scaled = grad * gain
    inner = (
        scaled
        - jnp.mean(scaled, -1, keepdims=True)
        - normed * jnp.mean(scaled * normed, -1, keepdims=True)
    )
    return (inner * rstd, jnp.sum(grad * normed, 0), jnp.sum(grad, 0))


def conv_rows(rimmed, kernel):
    return lax.conv_general_dilated(
        rimmed,
        kernel,
        (1, 1),
        ((0, 0), (1, 1)),
        dimension_numbers=("NHWC", "HWIO", "NHWC"),
        preferred_element_type=jnp.float32,
    )


def exact_gelu(values):
    return jax.nn.gelu(values, approximate=False)


def body(
    image,
    conv_weight,
    gn_gain,
    gn_bias,
    embed_weight,
    embed_bias,
    ln1_gain,
    ln1_bias,
    qkv_weight,
    query_bias,
    value_bias,
    out_weight,
    out_bias,
    ln2_gain,
    ln2_bias,
    up_weight,
    up_bias,
    down_weight,
    down_bias,
    text_embed,
    text_len,
    cotangent,
):
    half_type = jnp.bfloat16
    full_type = jnp.float32
    channels = conv_weight.shape[1]
    pixels = image
    row_start = lax.axis_index("band") * image.shape[1]
    images_here = pixels.shape[0]
    rows = pixels.shape[1]
    row_live = (row_start + jnp.arange(rows) < GRID).astype(full_type)[None, :, None, None]
    pixels = pixels * row_live.astype(half_type)
    rimmed = padded(pixels, (("band", 1),), 1)
    wfull = conv_weight.astype(full_type)
    wcent = wfull - jnp.mean(wfull, 0)
    wscale = lax.rsqrt(jnp.mean(wcent * wcent, 0) + 1e-05)
    stand_full = wcent * wscale
    kernel = stand_full.astype(half_type).reshape(3, 3, channels, channels)
    feat = conv_rows(rimmed, kernel) * row_live
    per_group = channels // GROUPS
    entries = GRID * GRID * per_group
    grouped = feat.reshape(images_here, rows, GRID, GROUPS, per_group)
    sum_one = jnp.sum(grouped, (1, 2, 4))
    sum_two = jnp.sum(grouped * grouped, (1, 2, 4))
    sum_one, sum_two = lax.psum((sum_one, sum_two), "band")
    gmean = (sum_one / entries)[:, None, None, :, None]
    gvar = (sum_two / entries)[:, None, None, :, None] - gmean * gmean
    gscale = lax.rsqrt(gvar + 1e-05)
    zgroup = (grouped - gmean) * gscale
    zhat = zgroup.reshape(images_here, rows, GRID, channels)
    normed = zhat * gn_gain + gn_bias
    stem_out, stem_pull = jax.vjp(exact_gelu, normed)
    active = (stem_out * row_live).astype(half_type)
    embedded = (matmul(active.reshape(-1, channels), embed_weight) + embed_bias).astype(half_type)
    embedded = embedded.reshape(images_here, rows, GRID, D)
    embedded = lax.all_to_all(embedded, "band", split_axis=0, concat_axis=1, tiled=True)
    full_rows = embedded.shape[1]
    patches = embedded[:, :GRID].reshape(-1, PATCHES, D)
    seqs = patches.shape[0]
    seq_len = PATCHES + TEXT
    stream = jnp.concatenate([patches.astype(full_type), text_embed.astype(full_type)], 1).reshape(
        -1, D
    )
    hidden, nhat_one, rstd_one = norm_forward(stream, ln1_gain, ln1_bias)
    hidden = hidden.astype(half_type)
    projected = matmul(hidden, qkv_weight)
    query = (projected[:, :D] + query_bias).astype(half_type).reshape(seqs, seq_len, HEADS, HD)
    key = projected[:, D : 2 * D].astype(half_type).reshape(seqs, seq_len, HEADS, HD)
    value = (projected[:, 2 * D :] + value_bias).astype(half_type).reshape(seqs, seq_len, HEADS, HD)
    live_keys = jnp.arange(seq_len)[None, :] < (PATCHES + text_len)[:, None]
    scale = HD ** (-0.5)

    def scores_of(queries, keys):
        raw = jnp.einsum("bqhd,bkhd->bhqk", queries, keys, preferred_element_type=full_type) * scale
        return jnp.where(live_keys[:, None, None, :], raw, -1000000000.0)

    scores = scores_of(query, key)
    peak = jnp.max(scores, -1, keepdims=True)
    expd = jnp.exp(scores - peak)
    total = jnp.sum(expd, -1, keepdims=True)
    probs = expd / total
    log_total = peak + jnp.log(total)
    mixed = jnp.einsum(
        "bhqk,bkhd->bqhd", probs.astype(half_type), value, preferred_element_type=full_type
    )
    mixed = mixed.astype(half_type).reshape(-1, D)
    mid = stream + matmul(mixed, out_weight) + out_bias
    hidden2, nhat_two, rstd_two = norm_forward(mid, ln2_gain, ln2_bias)
    hidden2 = hidden2.astype(half_type)
    pre = matmul(hidden2, up_weight) + up_bias
    gelu_out, gelu_pull = jax.vjp(exact_gelu, pre)
    act = gelu_out.astype(half_type)
    final = mid + matmul(act, down_weight) + down_bias
    encoded = final.astype(half_type).reshape(seqs, seq_len, D)
    grad_out = cotangent.reshape(-1, D)
    grad_full = grad_out.astype(full_type)
    g_down_w = matmul(act.T, grad_out)
    g_down_b = jnp.sum(grad_full, 0)
    d_pre = gelu_pull(matmul(grad_out, down_weight.T))[0].astype(half_type)
    g_up_w = matmul(hidden2.T, d_pre)
    g_up_b = jnp.sum(d_pre.astype(full_type), 0)
    d_mid_norm, g_ln2_g, g_ln2_b = norm_backward(
        matmul(d_pre, up_weight.T), nhat_two, rstd_two, ln2_gain
    )
    d_mid = grad_full + d_mid_norm
    d_attn = d_mid.astype(half_type)
    g_out_w = matmul(mixed.T, d_attn)
    g_out_b = jnp.sum(d_attn.astype(full_type), 0)
    d_mixed = matmul(d_attn, out_weight.T).astype(half_type).reshape(seqs, seq_len, HEADS, HD)
    probs_again = jnp.exp(scores_of(query, key) - log_total)
    d_probs = jnp.einsum("bqhd,bkhd->bhqk", d_mixed, value, preferred_element_type=full_type)
    d_value = jnp.einsum(
        "bhqk,bqhd->bkhd", probs_again.astype(half_type), d_mixed, preferred_element_type=full_type
    )
    delta = jnp.sum(d_probs * probs_again, -1, keepdims=True)
    d_scores = (probs_again * (d_probs - delta)).astype(half_type)
    d_query = jnp.einsum("bhqk,bkhd->bqhd", d_scores, key, preferred_element_type=full_type) * scale
    d_key = jnp.einsum("bhqk,bqhd->bkhd", d_scores, query, preferred_element_type=full_type) * scale
    d_qkv = jnp.concatenate(
        [d_query.reshape(-1, D), d_key.reshape(-1, D), d_value.reshape(-1, D)], 1
    ).astype(half_type)
    g_qkv_w = matmul(hidden.T, d_qkv)
    g_q_b = jnp.sum(d_qkv[:, :D].astype(full_type), 0)
    g_v_b = jnp.sum(d_qkv[:, 2 * D :].astype(full_type), 0)
    d_stream_norm, g_ln1_g, g_ln1_b = norm_backward(
        matmul(d_qkv, qkv_weight.T), nhat_one, rstd_one, ln1_gain
    )
    d_stream = (d_mid + d_stream_norm).reshape(seqs, seq_len, D)
    text_grad = d_stream[:, PATCHES:]
    d_patches = d_stream[:, :PATCHES].astype(half_type).reshape(seqs, GRID, GRID, D)
    d_grid = jnp.pad(d_patches, ((0, 0), (0, full_rows - GRID), (0, 0), (0, 0)))
    d_grid = lax.all_to_all(d_grid, "band", split_axis=1, concat_axis=0, tiled=True)
    flat_grad = d_grid.reshape(-1, D)
    g_emb_w = matmul(active.reshape(-1, channels).T, flat_grad)
    g_emb_b = jnp.sum(flat_grad.astype(full_type), 0)
    d_active = (
        matmul(flat_grad, embed_weight.T)
        .astype(half_type)
        .reshape(images_here, rows, GRID, channels)
    )
    d_norm = stem_pull(d_active.astype(full_type))[0] * row_live
    g_gn_g = jnp.sum(d_norm * zhat, (0, 1, 2))
    g_gn_b = jnp.sum(d_norm, (0, 1, 2))
    d_hat = (d_norm * gn_gain).reshape(images_here, rows, GRID, GROUPS, per_group)
    back_one = jnp.sum(d_hat, (1, 2, 4))
    back_two = jnp.sum(d_hat * zgroup, (1, 2, 4))
    back_one, back_two = lax.psum((back_one, back_two), "band")
    d_feat = gscale * (
        d_hat
        - (back_one / entries)[:, None, None, :, None]
        - zgroup * (back_two / entries)[:, None, None, :, None]
    )
    d_feat = (d_feat.reshape(images_here, rows, GRID, channels) * row_live).astype(half_type)
    widened = jnp.pad(rimmed, ((0, 0), (0, 0), (1, 1), (0, 0)))
    flat_feat = d_feat.reshape(-1, channels)
    windows = []
    for shift_r in range(3):
        for shift_c in range(3):
            window = widened[:, shift_r : shift_r + rows, shift_c : shift_c + GRID, :].reshape(
                -1, channels
            )
            windows.append(matmul(window.T, flat_feat))
    g_stand = jnp.concatenate(windows, 0)
    g_conv = wscale * (
        g_stand - jnp.mean(g_stand, 0) - stand_full * jnp.mean(g_stand * stand_full, 0)
    )
    flipped = jnp.flip(kernel, (0, 1)).transpose(0, 1, 3, 2)
    d_rim = padded(d_feat, (("band", 1),), 1)
    image_grad = conv_rows(d_rim, flipped) * row_live
    shares = (
        lax.psum_scatter(g_conv, "img", scatter_dimension=0, tiled=True),
        lax.psum_scatter(g_gn_g, "img", scatter_dimension=0, tiled=True),
        lax.psum_scatter(g_gn_b, "img", scatter_dimension=0, tiled=True),
        lax.psum_scatter(g_emb_w, "img", scatter_dimension=0, tiled=True),
        lax.psum_scatter(g_emb_b, "img", scatter_dimension=0, tiled=True),
        lax.psum_scatter(g_ln1_g, "img", scatter_dimension=0, tiled=True),
        lax.psum_scatter(g_ln1_b, "img", scatter_dimension=0, tiled=True),
        lax.psum_scatter(g_qkv_w, "img", scatter_dimension=0, tiled=True),
        lax.psum_scatter(g_q_b, "img", scatter_dimension=0, tiled=True),
        lax.psum_scatter(g_v_b, "img", scatter_dimension=0, tiled=True),
        lax.psum_scatter(g_out_w, "img", scatter_dimension=1, tiled=True),
        lax.psum_scatter(g_out_b, "img", scatter_dimension=0, tiled=True),
        lax.psum_scatter(g_ln2_g, "img", scatter_dimension=0, tiled=True),
        lax.psum_scatter(g_ln2_b, "img", scatter_dimension=0, tiled=True),
        lax.psum_scatter(g_up_w, "img", scatter_dimension=0, tiled=True),
        lax.psum_scatter(g_up_b, "img", scatter_dimension=0, tiled=True),
        lax.psum_scatter(g_down_w, "img", scatter_dimension=1, tiled=True),
        lax.psum_scatter(g_down_b, "img", scatter_dimension=0, tiled=True),
    )
    s_conv, s_emb, s_qkv, s_out, s_up, s_down = (
        lax.psum_scatter(shares[0], "band", scatter_dimension=1, tiled=True),
        lax.psum_scatter(shares[3], "band", scatter_dimension=1, tiled=True),
        lax.psum_scatter(shares[7], "band", scatter_dimension=1, tiled=True),
        lax.psum_scatter(shares[10], "band", scatter_dimension=0, tiled=True),
        lax.psum_scatter(shares[14], "band", scatter_dimension=1, tiled=True),
        lax.psum_scatter(shares[16], "band", scatter_dimension=0, tiled=True),
    )
    vectors = (
        shares[1],
        shares[2],
        shares[4],
        shares[5],
        shares[6],
        shares[8],
        shares[9],
        shares[11],
        shares[12],
        shares[13],
        shares[15],
        shares[17],
    )
    vsum = lax.psum(
        (
            vectors[0],
            vectors[1],
            vectors[2],
            vectors[3],
            vectors[4],
            vectors[5],
            vectors[6],
            vectors[7],
            vectors[8],
            vectors[9],
            vectors[10],
            vectors[11],
        ),
        "band",
    )
    summed = (
        s_conv,
        vsum[0],
        vsum[1],
        s_emb,
        vsum[2],
        vsum[3],
        vsum[4],
        s_qkv,
        vsum[5],
        vsum[6],
        s_out,
        vsum[7],
        vsum[8],
        vsum[9],
        s_up,
        vsum[10],
        s_down,
        vsum[11],
    )
    return (encoded, image_grad, text_grad) + summed


def solution(mesh):
    in_specs = (
        P("img", "band", None, None),
        P(),
        P(),
        P(),
        P(),
        P(),
        P(),
        P(),
        P(),
        P(),
        P(),
        P(),
        P(),
        P(),
        P(),
        P(),
        P(),
        P(),
        P(),
        P(("img", "band"), None, None),
        P(("img", "band")),
        P(("img", "band"), None, None),
    )
    out_specs = (
        P(("img", "band"), None, None),
        P("img", "band", None, None),
        P(("img", "band"), None, None),
        P("img", "band"),
        P("img"),
        P("img"),
        P("img", "band"),
        P("img"),
        P("img"),
        P("img"),
        P("img", "band"),
        P("img"),
        P("img"),
        P("band", "img"),
        P("img"),
        P("img"),
        P("img"),
        P("img", "band"),
        P("img"),
        P("band", "img"),
        P("img"),
    )
    return jax.shard_map(body, mesh=mesh, in_specs=in_specs, out_specs=out_specs, check_vma=False)
```

profile of v0, /device:TPU:0, one launch (start us, length us, event | category | flops | bytes accessed | tf_op | source)
XLA Modules:
  0.0 963.8 jit_solution(6772577458714462043)
XLA Ops:
  8.4 2.5 collective-permute-start
  21.1 2.5 fusion.164
  28.3 9.5 all-reduce.16
  41.9 1.9 fusion.81
  44.5 2.0 multiply_convert_fusion.2
  48.9 2.0 fusion.30
  50.9 1.8 reshape.350
  52.8 1.9 copy.151
  54.7 4.1 all-to-all-start
  59.7 6.1 all-to-all-done
  65.8 1.8 copy.152
  69.4 1.8 copy.153
  71.2 1.8 convert_element_type.135
  75.4 2.1 fusion.146
  79.3 1.9 copy.155
  81.2 1.9 copy.156
  83.2 1.9 copy.154
  85.1 1.9 fusion.165
  91.2 8.5 multiply_convert_fusion.1
  99.7 2.9 convert_reduce_fusion.1
  102.6 2.2 multiply_reduce_fusion.1
  107.9 1.9 copy.159
  109.9 2.6 fusion.25
  115.6 1.9 fusion.51
  118.8 9.8 %all_to_all.21 = bf16[1,16,14,768]{3,2,0,1:T(8,128)(2,1)S(1)} all-to-all(bf16[1,16,14,768]{3,2,0,1:T(8,128)(2,1)S(1)} %pad.8), channel_id=1, replica_groups=mesh['img'=8,'band'=4] {'band'}, dimensions={1} | all-to-all | bytes 688128 | tf_op jit(solution)/shard_map/all_to_all | solution.py:201
  130.1 4.3 fusion.55
  140.8 1.9 fusion.140
  144.1 38.0 %all-reduce.14 = (f32[256]{0:T(256)S(1)}, f32[256]{0:T(256)S(1)}, f32[768]{0:T(1024)S(1)}, f32[768]{0:T(1024)S(1)}, f32[768]{0:T(1024)S(1)}, /*index=5*/f32[768]...) all-reduce(f32[256]{0:T(256)S(1)} %get-tuple-element.113, ...), channel_id=4, replica_groups=mesh['img'=8,'band'=4] {'img'}, use_global_device_ids=true, to_apply=%region_38.39.clone | all-reduce | flops 10496 | bytes 83968
  183.4 11.1 %all-reduce.15 = (f32[4,32]{1,0:T(4,128)S(1)}, f32[4,32]{1,0:T(4,128)S(1)}, f32[32]{0:T(128)}, f32[32]{0:T(128)}, f32[96]{0:T(128)}, /*index=5*/f32[96]{0:T(128)...) all-reduce(f32[4,32]{1,0:T(4,128)S(1)} %reduce_sum.409, ...), channel_id=1, replica_groups=mesh['img'=8,'band'=4] {'band'}, use_global_device_ids=true, to_apply=%region_24.25 | all-reduce | flops 1568 | bytes 12544 | tf_op jit(solution)/shard_map/psum | solution.py:216
  199.9 2.1 fusion.14
  203.8 5.3 fusion.148
  210.5 5.1 fusion.69
  217.6 107.6 %reduce-scatter.25.cloned.1.call-done = f32[96,2304]{1,0:T(8,128)} async-done(((f32[768,2304]{1,0:T(8,128)}), f32[96,2304]{1,0:T(8,128)}) %reduce-scatter.25.cloned.1.call-update) | async-done | bytes 884752 | tf_op jit(solution)/shard_map/reduce_scatter | solution.py:247
  325.2 2.6 copy.202
  327.8 69.0 %reduce-scatter.27.cloned.1.call-done = f32[768,96]{0,1:T(8,128)} async-done(((f32[768,768]{0,1:T(8,128)}), f32[768,96]{0,1:T(8,128)}) %reduce-scatter.27.cloned.1.call-update) | async-done | bytes 294928 | tf_op jit(solution)/shard_map/reduce_scatter | solution.py:250
  396.8 1.9 copy.204
  398.8 69.4 %reduce-scatter.21.cloned.1.call-done = f32[288,256]{1,0:T(8,128)} async-done(((f32[2304,256]{1,0:T(8,128)}), f32[288,256]{1,0:T(8,128)}) %reduce-scatter.21.cloned.1.call-update) | async-done | bytes 294928 | tf_op jit(solution)/shard_map/reduce_scatter | solution.py:240
  468.2 1.9 copy.198
  470.2 163.8 %reduce-scatter.29.cloned.1.call-done = f32[96,3072]{1,0:T(8,128)} async-done(((f32[768,3072]{1,0:T(8,128)}), f32[96,3072]{1,0:T(8,128)}) %reduce-scatter.29.cloned.1.call-update) | async-done | bytes 1179664 | tf_op jit(solution)/shard_map/reduce_scatter | solution.py:254
  634.1 165.8 %reduce-scatter.33.cloned.1.call-done = f32[3072,96]{0,1:T(8,128)} async-done(((f32[3072,768]{0,1:T(8,128)}), f32[3072,96]{0,1:T(8,128)}) %reduce-scatter.33.cloned.1.call-update) | async-done | bytes 1179664 | tf_op jit(solution)/shard_map/reduce_scatter | solution.py:256
  803.3 4.4 fusion.31
  811.1 11.3 %reduce-scatter.39.cloned.1.call-done = f32[192,32]{1,0:T(8,128)} async-done(((f32[768,32]{1,0:T(8,128)}), f32[192,32]{1,0:T(8,128)}) %reduce-scatter.39.cloned.1.call-update) | async-done | bytes 24592
  824.0 26.7 %reduce-scatter.41.cloned.1.call-done = f32[576,96]{1,0:T(8,128)} async-done(((f32[2304,96]{1,0:T(8,128)}), f32[576,96]{1,0:T(8,128)}) %reduce-scatter.41.cloned.1.call-update) | async-done | bytes 221200
  850.7 1.8 copy.203
  852.5 22.3 %reduce-scatter.43.cloned.1.call-done = f32[192,96]{1,0:T(8,128)} async-done(((f32[768,96]{1,0:T(8,128)}), f32[192,96]{1,0:T(8,128)}) %reduce-scatter.43.cloned.1.call-update) | async-done | bytes 73744
  874.8 23.9 %reduce-scatter.37.cloned.1.call-done = f32[64,288]{1,0:T(8,128)} async-done(((f32[256,288]{1,0:T(8,128)}), f32[64,288]{1,0:T(8,128)}) %reduce-scatter.37.cloned.1.call-update) | async-done | bytes 73744
  898.7 29.0 %reduce-scatter.31.cloned.1.call-done = f32[96,768]{1,0:T(8,128)} async-done(((f32[96,3072]{1,0:T(8,128)}), f32[96,768]{1,0:T(8,128)}) %reduce-scatter.31.cloned.1.call-update) | async-done | bytes 294928 | tf_op jit(solution)/shard_map/reduce_scatter | solution.py:264
  927.7 28.7 %reduce-scatter.35.cloned.1.call-done = f32[768,96]{0,1:T(8,128)} async-done(((f32[3072,96]{0,1:T(8,128)}), f32[768,96]{0,1:T(8,128)}) %reduce-scatter.35.cloned.1.call-update) | async-done | bytes 294928 | tf_op jit(solution)/shard_map/reduce_scatter | solution.py:265
  (369 shorter events, 67.5 us)
Async XLA Ops:
  7.2 68.2 %copy-start = (bf16[768,2304]{1,0:T(8,128)(2,1)S(1)}, bf16[768,2304]{1,0:T(8,128)(2,1)}, u32[]{:S(2)}) copy-start(bf16[768,2304]{1,0:T(8,128)(2,1)} %param.30) | copy-start | bytes 10616836
  7.2 8.3 copy-start.4
  8.4 8.5 copy-start.48
  8.4 8.4 collective-permute-start
  10.9 6.0 collective-permute-start.1
  13.8 7.2 copy-start.100
  16.9 26.9 %copy-start.86 = (f32[4]{0:T(128)}, f32[4]{0:T(128)S(1)}, u32[]{:S(2)}) copy-start(f32[4]{0:T(128)S(1)} %compare_convert_fusion) | copy-start | bytes 52
  21.1 20.8 %copy-start.79 = (f32[256]{0:T(256)S(1)}, f32[256]{0:T(256)}, u32[]{:S(2)}) copy-start(f32[256]{0:T(256)} %param.24) | copy-start | bytes 3076
  41.8 7.2 copy-start.63
  50.9 24.5 %copy-start.54 = (f32[768]{0:T(1024)S(1)}, f32[768]{0:T(1024)}, u32[]{:S(2)}) copy-start(f32[768]{0:T(1024)} %param.28) | copy-start | bytes 9220
  50.9 24.5 %copy-start.57 = (f32[768]{0:T(1024)S(1)}, f32[768]{0:T(1024)}, u32[]{:S(2)}) copy-start(f32[768]{0:T(1024)} %param.29) | copy-start | bytes 9220
  54.7 11.1 %all-to-all-start = ((bf16[4,4,14,768]{3,1,2,0:T(4,128)(2,1)}), bf16[4,4,14,768]{3,1,2,0:T(4,128)(2,1)}, u32[]{:S(2)}, u32[]{:S(2)}) async-start(bf16[4,4,14,768]{3,1,2,0:T(4,128)(2,1)} %copy.151), calls=%async_computation | async-start | bytes 688128 | tf_op jit(solution)/shard_map/all_to_all | solution.py:125
  58.8 156.9 %reduce-scatter.23.cloned.1.call-start = ((), (), s32[]{:S(2)}) async-start(), calls=%async_computation.15 | async-start | bytes 884736 | tf_op jit(solution)/shard_map/reduce_scatter | solution.py:243
  90.3 9.4 slice-start.2
  90.9 14.0 %copy-start.12 = (f32[228,768]{1,0:T(8,128)}, f32[228,768]{1,0:T(8,128)S(1)}, u32[]{:S(2)}) copy-start(f32[228,768]{1,0:T(8,128)S(1)} %get-tuple-element.189) | copy-start | bytes 2101252
  90.9 13.9 %copy-start.71 = (f32[228]{0:T(256)}, f32[228]{0:T(256)S(1)}, u32[]{:S(2)}) copy-start(f32[228]{0:T(256)S(1)} %broadcast_multiply_fusion.7) | copy-start | bytes 2740
  91.2 13.6 %copy-start.77 = (f32[228]{0:T(256)}, f32[228]{0:T(256)S(1)}, u32[]{:S(2)}) copy-start(f32[228]{0:T(256)S(1)} %add_rsqrt_fusion.1) | copy-start | bytes 2740
  91.2 8.5 copy-start.30
  91.2 8.5 slice-start.3
  117.6 11.2 %copy-start.42 = (bf16[224,256]{1,0:T(8,128)(2,1)S(1)}, bf16[224,256]{1,0:T(8,128)(2,1)}, u32[]{:S(2)}) copy-start(bf16[224,256]{1,0:T(8,128)(2,1)} %reshape.349) | copy-start | bytes 344068
  117.9 12.1 %copy-start.11 = (bf16[1,196,768]{2,1,0:T(8,128)(2,1)S(1)}, bf16[1,196,768]{2,1,0:T(8,128)(2,1)}, u32[]{:S(2)}) copy-start(bf16[1,196,768]{2,1,0:T(8,128)(2,1)} %convert_element_type.135) | copy-start | bytes 903172
  117.9 12.1 %copy-start.17 = (bf16[12,64,228]{2,1,0:T(8,128)(2,1)S(1)}, bf16[12,64,228]{2,1,0:T(8,128)(2,1)}, u32[]{:S(2)}) copy-start(bf16[12,64,228]{2,1,0:T(8,128)(2,1)} %copy-done.16) | copy-start | bytes 1050628
  118.0 12.1 %copy-start.19 = (bf16[12,64,228]{2,1,0:T(8,128)(2,1)S(1)}, bf16[12,64,228]{2,1,0:T(8,128)(2,1)}, u32[]{:S(2)}) copy-start(bf16[12,64,228]{2,1,0:T(8,128)(2,1)} %copy-done.18) | copy-start | bytes 1050628
  118.0 12.1 %copy-start.26 = (bf16[12,64,228]{2,1,0:T(8,128)(2,1)S(1)}, bf16[12,64,228]{2,1,0:T(8,128)(2,1)}, u32[]{:S(2)}) copy-start(bf16[12,64,228]{2,1,0:T(8,128)(2,1)} %copy-done.25) | copy-start | bytes 1050628
  118.0 12.1 %copy-start.36 = (bf16[1,32,768]{2,1,0:T(8,128)(2,1)S(1)}, bf16[1,32,768]{2,1,0:T(8,128)(2,1)}, u32[]{:S(2)}) copy-start(bf16[1,32,768]{2,1,0:T(8,128)(2,1)} %param.41) | copy-start | bytes 147460
  118.0 12.1 %copy-start.58 = (f32[768]{0:T(1024)S(1)}, f32[768]{0:T(1024)}, u32[]{:S(2)}) copy-start(f32[768]{0:T(1024)} %param.29) | copy-start | bytes 9220
  130.0 195.2 %reduce-scatter.25.cloned.1.call-start = ((), (), s32[]{:S(2)}) async-start(), calls=%async_computation.16 | async-start | bytes 7962624 | tf_op jit(solution)/shard_map/reduce_scatter | solution.py:247
  134.4 262.4 %reduce-scatter.27.cloned.1.call-start = ((), (), s32[]{:S(2)}) async-start(), calls=%async_computation.17 | async-start | bytes 2654208 | tf_op jit(solution)/shard_map/reduce_scatter | solution.py:250
  142.8 52.4 %copy-start.64 = (f32[4,256]{1,0:T(4,128)S(1)}, f32[4,256]{1,0:T(4,128)}, u32[]{:S(2)}) copy-start(f32[4,256]{1,0:T(4,128)} %copy-done.63) | copy-start | bytes 12292
  142.8 325.4 %reduce-scatter.21.cloned.1.call-start = ((), (), s32[]{:S(2)}) async-start(), calls=%async_computation.14 | async-start | bytes 2654208 | tf_op jit(solution)/shard_map/reduce_scatter | solution.py:240
  144.0 52.6 %copy-start.49 = (bf16[4,4,14,256]{3,2,1,0:T(8,128)(2,1)S(1)}, bf16[4,4,14,256]{3,2,1,0:T(8,128)(2,1)}, u32[]{:S(2)}) copy-start(bf16[4,4,14,256]{3,2,1,0:T(8,128)(2,1)} %copy-done.48) | copy-start | bytes 344068
  144.0 52.7 %copy-start.70 = (bf16[4,1,14,256]{3,2,1,0:T(8,128)(2,1)S(1)}, bf16[4,1,14,256]{3,2,1,0:T(8,128)(2,1)}, u32[]{:S(2)}) copy-start(bf16[4,1,14,256]{3,2,1,0:T(8,128)(2,1)} %copy-done.69) | copy-start | bytes 86020
  202.0 432.0 %reduce-scatter.29.cloned.1.call-start = ((), (), s32[]{:S(2)}) async-start(), calls=%async_computation.18 | async-start | bytes 10616832 | tf_op jit(solution)/shard_map/reduce_scatter | solution.py:254
  209.1 590.8 %reduce-scatter.33.cloned.1.call-start = ((), (), s32[]{:S(2)}) async-start(), calls=%async_computation.20 | async-start | bytes 10616832 | tf_op jit(solution)/shard_map/reduce_scatter | solution.py:256
  215.6 606.8 %reduce-scatter.39.cloned.1.call-start = ((), (), s32[]{:S(2)}) async-start(), calls=%async_computation.23 | async-start | bytes 491520
  217.5 633.1 %reduce-scatter.41.cloned.1.call-start = ((), (), s32[]{:S(2)}) async-start(), calls=%async_computation.24 | async-start | bytes 1474560
  327.8 472.2 %copy-start.44 = (bf16[4,4,14,256]{3,1,2,0:T(4,128)(2,1)S(1)}, bf16[4,4,14,256]{3,1,2,0:T(4,128)(2,1)}, u32[]{:S(2)}) copy-start(bf16[4,4,14,256]{3,1,2,0:T(4,128)(2,1)} %copy-done.43) | copy-start | bytes 344068
  327.8 475.5 %copy-start.98 = (f32[768]{0:T(1024)S(1)}, f32[768]{0:T(1024)}, u32[]{:S(2)}) copy-start(f32[768]{0:T(1024)} %param.40) | copy-start | bytes 9220
  327.8 547.0 %reduce-scatter.43.cloned.1.call-start = ((), (), s32[]{:S(2)}) async-start(), calls=%async_computation.25 | async-start | bytes 491520
  398.7 500.0 %reduce-scatter.37.cloned.1.call-start = ((), (), s32[]{:S(2)}) async-start(), calls=%async_computation.22 | async-start | bytes 491520
  470.2 457.6 %reduce-scatter.31.cloned.1.call-start = ((), (), s32[]{:S(2)}) async-start(), calls=%async_computation.19 | async-start | bytes 1474560 | tf_op jit(solution)/shard_map/reduce_scatter | solution.py:264
  634.1 322.4 %reduce-scatter.35.cloned.1.call-start = ((), (), s32[]{:S(2)}) async-start(), calls=%async_computation.21 | async-start | bytes 1474560 | tf_op jit(solution)/shard_map/reduce_scatter | solution.py:265
  800.0 9.2 collective-permute-start.2
  801.8 7.8 copy-start.38
  801.8 7.8 copy-start.88
  801.8 7.8 copy-start.101
  801.9 7.4 collective-permute-start.3
  809.4 147.0 %copy-start.1 = (bf16[768,2304]{1,0:T(8,128)(2,1)S(1)}, bf16[768,2304]{1,0:T(8,128)(2,1)}, u32[]{:S(2)}) copy-start(bf16[768,2304]{1,0:T(8,128)(2,1)} %param.30) | copy-start | bytes 10616836
  (75 other events, 164.2 us)
Sparse Core Ops, SparseCore 0:
  130.1 62.8 reduce-scatter.22
  197.1 128.0 reduce-scatter.24
  328.7 68.0 reduce-scatter.26
  400.1 68.0 reduce-scatter.20
  471.7 162.3 reduce-scatter.28
  637.5 162.3 reduce-scatter.32
  802.4 19.9 reduce-scatter.38
  824.9 25.6 reduce-scatter.40
  853.9 20.8 reduce-scatter.42
  877.8 20.8 reduce-scatter.36
  902.0 25.6 reduce-scatter.30
  930.7 25.7 reduce-scatter.34
where the time goes:
time: 970 us; the launch traced here: 964 us
  waiting for transfers between devices  724 us (75%)
  blocking collectives  68.4 us (7%)
  local copies, waits for them, and re-layouts  60.4 us (6%)
  matrix products  57 us (6%)
  other arithmetic  23 us (2%)
  between operations  18.9 us (2%)
  starting transfers between devices  12 us (1%)
    reduce_scatter x1, waiting for transfers between devices, body(): lax.psum_scatter(g_down_w, 'img', scatter_dimension=1, tiled=True)  166 us
    reduce_scatter x1, waiting for transfers between devices, body(): lax.psum_scatter(g_up_w, 'img', scatter_dimension=0, tiled=True)  164 us
    reduce_scatter x1, waiting for transfers between devices, body(): lax.psum_scatter(g_qkv_w, 'img', scatter_dimension=0, tiled=True)  108 us
    unnamed x16, waiting for transfers between devices  84.4 us
    reduce_scatter x1, waiting for transfers between devices, body(): lax.psum_scatter(g_conv, 'img', scatter_dimension=0, tiled=True)  69.4 us
    reduce_scatter x1, waiting for transfers between devices, body(): lax.psum_scatter(g_out_w, 'img', scatter_dimension=1, tiled=True)  69 us
    dot_general x24, matrix products, matmul(): return jnp.dot(left, right, preferred_element_type=jnp.float32)  47.1 us
    unnamed x1, blocking collectives  38 us
  transfers between devices with their start and end apart: 17, of which 12 were waited for; matrix products, arithmetic and copies ran while one was open for 5% of the time, Pallas kernels for 0%

commit v1 on v0

--- a/solution.py
+++ b/solution.py
@@ -1,6 +1,10 @@
+import functools
+
 import jax
 import jax.numpy as jnp
 from jax import lax
+from jax.experimental import pallas as pl
+from jax.experimental.pallas import tpu as pltpu
 from jax.sharding import PartitionSpec as P
 
 D = 768
@@ -10,6 +14,288 @@
 GRID = 14
 TEXT = 32
 PATCHES = 196
+
+
+MESH_ID = pl.DeviceIdType.MESH
+HALF = jnp.bfloat16
+FULL = jnp.float32
+TOK = 256
+
+
+def bit_of(value, bit):
+    return lax.rem(lax.div(value, bit), 2)
+
+
+def flip(value, bit):
+    return value + bit * (1 - 2 * bit_of(value, bit))
+
+
+def partner(label):
+    axis, bit = label
+    img, band = lax.axis_index("img"), lax.axis_index("band")
+    return (flip(img, bit), band) if axis == "img" else (img, flip(band, bit))
+
+
+def my_bit(label):
+    axis, bit = label
+    return bit_of(lax.axis_index(axis), bit)
+
+
+def bits(count):
+    return [1 << k for k in range(count.bit_length() - 1)]
+
+
+class Plan:
+    def __init__(self, n_img, rows, width, lead, order):
+        self.width = width
+        split = [("img", k) for k in reversed(bits(n_img)) if (rows // n_img) * k % 16 == 0]
+        self.rows = rows >> len(split)
+        self.first = ([lead] if lead else []) + split
+        rest = [("img", k) for k in bits(n_img) if ("img", k) not in split]
+        ordered = [lab for lab in order if lab in self.first]
+        self.order = ordered + rest + [lab for lab in order if lab not in self.first and lab[0] == "band"]
+        self.shapes = []
+        labels = list(self.first)
+        for lab in self.order:
+            if lab in labels:
+                labels.remove(lab)
+            self.shapes.append((2,) * len(labels) + (self.rows, width))
+        self.shape = (2,) * len(self.first) + (self.rows, width)
+
+    def scratch(self, kind):
+        return [pltpu.VMEM(s, kind) for s in [self.shape] + self.shapes]
+
+
+class Piece:
+    def __init__(self, plan, refs, sems, slot):
+        self.plan, self.buf, self.recv = plan, refs[0], refs[1:]
+        self.sems, self.slot = sems, slot
+        self.labels, self.cur = list(plan.first), refs[0]
+        self.sent = []
+
+    def _index(self, label, which):
+        at = self.labels.index(label)
+        return (slice(None),) * at + (which,)
+
+    def start(self, stage):
+        label = self.plan.order[stage]
+        src = self.cur
+        if label in self.labels:
+            src = src.at[self._index(label, 1 - my_bit(label))]
+        send, recv = self.sems
+        copy = pltpu.make_async_remote_copy(
+            src_ref=src,
+            dst_ref=self.recv[stage],
+            send_sem=send.at[self.slot + stage],
+            recv_sem=recv.at[self.slot + stage],
+            device_id=partner(label),
+            device_id_type=MESH_ID,
+        )
+        copy.start()
+        self.sent.append(copy)
+
+    def finish(self, stage, out=None):
+        label = self.plan.order[stage]
+        self.sent[stage].wait_recv()
+        mine = self.cur
+        if label in self.labels:
+            mine = mine[self._index(label, my_bit(label))]
+            self.labels.remove(label)
+        else:
+            mine = mine[...]
+        got = self.recv[stage]
+        if out is None:
+            got[...] = got[...] + mine
+        else:
+            out[...] = (got[...].astype(FULL) + mine.astype(FULL)).reshape(out.shape)
+        self.cur = got
+
+    def drain(self):
+        for copy in self.sent:
+            copy.wait_send()
+
+
+def dot_tn(left, right):
+    return lax.dot_general(left, right, (((0,), (0,)), ((), ())), preferred_element_type=FULL)
+
+
+def grads_kernel(plans, vec_rows, *refs):
+    (cot, act, hid2, dpre, dattn, mixed, hid, dqkv, win, dfeat, active, dpat, vec,
+     o_down, o_up, o_out, o_qkv, o_conv, o_emb, o_vec) = refs[:20]
+    rest = list(refs[20:])
+    (r_cot, r_act, r_hid2, r_dpre, r_dattn, r_mixed, r_hid, r_dqkv, r_win, r_dfeat, r_active, r_dpat) = rest[:12]
+    rest = rest[12:]
+    core_send, core_recv, send_sem, recv_sem = rest[-4:]
+    rest = rest[:-4]
+    pieces = []
+    slot = 0
+    for plan in plans:
+        count = 1 + len(plan.order)
+        pieces.append(Piece(plan, rest[:count], (send_sem, recv_sem), slot))
+        rest = rest[count:]
+        slot += count - 1
+    vec_recv = rest
+    core = ("band", 1)
+    links = [core, ("band", 2)] + [("img", k) for k in bits(lax.axis_size("img"))]
+    barrier = pltpu.get_barrier_semaphore()
+    for label in links:
+        pl.semaphore_signal(barrier, inc=1, device_id=partner(label), device_id_type=MESH_ID)
+    pl.semaphore_wait(barrier, len(links))
+    c = my_bit(core)
+    core_copies = {}
+
+    def swap(name, at, src, dst):
+        copy = pltpu.make_async_remote_copy(
+            src_ref=src, dst_ref=dst, send_sem=core_send.at[at], recv_sem=core_recv.at[at],
+            device_id=partner(core), device_id_type=MESH_ID)
+        copy.start()
+        core_copies.setdefault(name, []).append(copy)
+
+    def swap_bands(name, at, src, dst):
+        for y in range(2):
+            swap(name, at + y, src.at[2 * y + 1 - c], dst.at[y])
+
+    swap("down", 0, cot, r_cot)
+    swap_bands("down", 1, act, r_act)
+    swap("up", 3, hid2, r_hid2)
+    swap_bands("up", 4, dpre, r_dpre)
+    swap("qkv", 6, hid, r_hid)
+    swap_bands("qkv", 7, dqkv, r_dqkv)
+    swap("out", 9, dattn, r_dattn)
+    swap_bands("out", 10, mixed, r_mixed)
+    swap("conv", 12, win, r_win)
+    swap("conv", 13, dfeat, r_dfeat)
+    swap("emb", 14, active, r_active)
+    swap("emb", 15, dpat, r_dpat)
+
+    def arrived(name):
+        for copy in core_copies[name]:
+            copy.wait_recv()
+
+    def store(piece, y, value):
+        shape = piece.plan.shape
+        if y is None:
+            piece.buf[...] = value.astype(HALF).reshape(shape)
+        else:
+            piece.buf[y] = value.astype(HALF).reshape(shape[1:])
+
+    def unit(name, left, r_left, right, r_right, parts):
+        arrived(name)
+        for piece, lo in parts:
+            w = piece.plan.width
+            for y in range(2):
+                for at in range(0, w, 128):
+                    wide = slice(lo + at, lo + at + 128)
+                    value = dot_tn(left[...], right[2 * y + c, :, wide])
+                    value += dot_tn(r_left[...], r_right[y, :, wide])
+                    value = value.astype(HALF).reshape(piece.plan.shape[1:-1] + (128,))
+                    lead = (y,) + (slice(None),) * (len(piece.plan.shape) - 2)
+                    piece.buf[lead + (slice(at, at + 128),)] = value
+            piece.start(0)
+
+    def columns(values, width):
+        total = values.shape[1]
+        row = lax.broadcasted_iota(jnp.int32, (total, 2 * width), 0)
+        col = lax.broadcasted_iota(jnp.int32, (total, 2 * width), 1)
+        want = jnp.where(col < width, col + c * width, col + width + c * width)
+        pick = jnp.where(row == want, 1.0, 0.0).astype(HALF)
+        return jnp.dot(values, pick, preferred_element_type=FULL).astype(HALF)
+
+    p_da, p_db, p_ua, p_ub, p_qa, p_qb, p_o, p_c, p_e = pieces
+    half = p_da.plan.width
+    unit("down", cot, r_cot, act, r_act, [(p_da, 0), (p_db, half)])
+    unit("up", hid2, r_hid2, dpre, r_dpre, [(p_ua, 0), (p_ub, half)])
+    unit("qkv", hid, r_hid, dqkv, r_dqkv, [(p_qa, 0), (p_qb, p_qa.plan.width)])
+    unit("out", dattn, r_dattn, mixed, r_mixed, [(p_o, 0)])
+    arrived("conv")
+    mine, theirs = columns(dfeat[...], 64), columns(r_dfeat[...], 64)
+    store(p_c, None, dot_tn(win[...], mine) + dot_tn(r_win[...], theirs))
+    p_c.start(0)
+    arrived("emb")
+    mine, theirs = columns(dpat[...], 192), columns(r_dpat[...], 192)
+    store(p_e, None, dot_tn(active[...], mine) + dot_tn(r_active[...], theirs))
+    p_e.start(0)
+    o_vec[...] = vec[...]
+    vec_copies = []
+
+    def vec_start(stage):
+        copy = pltpu.make_async_remote_copy(
+            src_ref=vec_recv[2 * stage], dst_ref=vec_recv[2 * stage + 1],
+            send_sem=send_sem.at[slot + stage], recv_sem=recv_sem.at[slot + stage],
+            device_id=partner(links[stage]), device_id_type=MESH_ID)
+        copy.start()
+        vec_copies.append(copy)
+
+    vec_recv[0][...] = vec[...]
+    vec_start(0)
+    outs = {id(p_da): (o_down, 0), id(p_db): (o_down, half), id(p_ua): (o_up, 0), id(p_ub): (o_up, half),
+            id(p_qa): (o_qkv, 0), id(p_qb): (o_qkv, p_qa.plan.width), id(p_o): (o_out, 0), id(p_c): (o_conv, 0), id(p_e): (o_emb, 0)}
+    deepest = max(len(p.plan.order) for p in pieces)
+    for stage in range(max(deepest, len(links))):
+        for piece in pieces:
+            if stage < len(piece.plan.order):
+                last = stage == len(piece.plan.order) - 1
+                ref, lo = outs[id(piece)]
+                piece.finish(stage, ref.at[:, pl.ds(lo, piece.plan.width)] if last else None)
+                if not last:
+                    piece.start(stage + 1)
+        if stage < len(links):
+            vec_copies[stage].wait_recv()
+            total = vec_recv[2 * stage][...] + vec_recv[2 * stage + 1][...]
+            if stage == len(links) - 1:
+                o_vec[...] = total
+            else:
+                vec_recv[2 * stage + 2][...] = total
+                vec_start(stage + 1)
+    for piece in pieces:
+        piece.drain()
+    for copy in vec_copies:
+        copy.wait_send()
+    for group in core_copies.values():
+        for copy in group:
+            copy.wait_send()
+
+
+def reduce_grads(cot, act, hid2, dpre, dattn, mixed, hid, dqkv, win, dfeat, active, dpat, vec):
+    n_img = lax.axis_size("img")
+    y = ("band", 2)
+    img_bits = [("img", k) for k in bits(n_img)]
+    y_first = [y] + img_bits
+    x_first = img_bits[:1] + [y] + img_bits[1:]
+    tail = img_bits + [y]
+    plans = [
+        Plan(n_img, D, 384, y, y_first),
+        Plan(n_img, D, 384, y, x_first),
+        Plan(n_img, D, 384, y, y_first),
+        Plan(n_img, D, 384, y, x_first),
+        Plan(n_img, D, 384, y, y_first),
+        Plan(n_img, D, 256, y, x_first),
+        Plan(n_img, D, 256, y, y_first),
+        Plan(n_img, win.shape[1], 128, None, tail),
+        Plan(n_img, active.shape[1], 384, None, tail),
+    ]
+    outs = [(plans[0].rows, D), (plans[2].rows, D), (plans[6].rows, 256), (plans[4].rows, 640), (plans[7].rows, 128), (plans[8].rows, 384), vec.shape]
+    half = lambda *s: pltpu.VMEM(s, HALF)
+    scratch = [half(TOK, D), half(2, TOK, D), half(TOK, D), half(2, TOK, D), half(TOK, D), half(2, TOK, 256),
+               half(TOK, D), half(2, TOK, 640), half(*win.shape), half(*dfeat.shape), half(*active.shape), half(*dpat.shape)]
+    slots = 0
+    for plan in plans:
+        scratch += plan.scratch(HALF)
+        slots += len(plan.order)
+    n_links = 2 + len(img_bits)
+    scratch += [pltpu.VMEM(vec.shape, FULL)] * (2 * n_links)
+    slots += n_links
+    scratch += [pltpu.SemaphoreType.DMA((16,)), pltpu.SemaphoreType.DMA((16,)), pltpu.SemaphoreType.DMA((slots,)), pltpu.SemaphoreType.DMA((slots,))]
+    vm = pl.BlockSpec(memory_space=pltpu.VMEM)
+    args = (cot, act, hid2, dpre, dattn, mixed, hid, dqkv, win, dfeat, active, dpat, vec)
+    return pl.pallas_call(
+        functools.partial(grads_kernel, plans, vec.shape[0]),
+        out_shape=[jax.ShapeDtypeStruct(s, FULL) for s in outs],
+        in_specs=[vm] * len(args),
+        out_specs=[vm] * len(outs),
+        scratch_shapes=scratch,
+        compiler_params=pltpu.CompilerParams(collective_id=0, has_side_effects=True, vmem_limit_bytes=60 * 2**20),
+    )(*args)
 
 
 def padded(cells, sides, width):
@@ -163,17 +449,14 @@
     encoded = final.astype(half_type).reshape(seqs, seq_len, D)
     grad_out = cotangent.reshape(-1, D)
     grad_full = grad_out.astype(full_type)
-    g_down_w = matmul(act.T, grad_out)
     g_down_b = jnp.sum(grad_full, 0)
     d_pre = gelu_pull(matmul(grad_out, down_weight.T))[0].astype(half_type)
-    g_up_w = matmul(hidden2.T, d_pre)
     g_up_b = jnp.sum(d_pre.astype(full_type), 0)
     d_mid_norm, g_ln2_g, g_ln2_b = norm_backward(
         matmul(d_pre, up_weight.T), nhat_two, rstd_two, ln2_gain
     )
     d_mid = grad_full + d_mid_norm
     d_attn = d_mid.astype(half_type)
-    g_out_w = matmul(mixed.T, d_attn)
     g_out_b = jnp.sum(d_attn.astype(full_type), 0)
     d_mixed = matmul(d_attn, out_weight.T).astype(half_type).reshape(seqs, seq_len, HEADS, HD)
     probs_again = jnp.exp(scores_of(query, key) - log_total)
@@ -188,7 +471,6 @@
     d_qkv = jnp.concatenate(
         [d_query.reshape(-1, D), d_key.reshape(-1, D), d_value.reshape(-1, D)], 1
     ).astype(half_type)
-    g_qkv_w = matmul(hidden.T, d_qkv)
     g_q_b = jnp.sum(d_qkv[:, :D].astype(full_type), 0)
     g_v_b = jnp.sum(d_qkv[:, 2 * D :].astype(full_type), 0)
     d_stream_norm, g_ln1_g, g_ln1_b = norm_backward(
@@ -200,7 +482,6 @@
     d_grid = jnp.pad(d_patches, ((0, 0), (0, full_rows - GRID), (0, 0), (0, 0)))
     d_grid = lax.all_to_all(d_grid, "band", split_axis=1, concat_axis=0, tiled=True)
     flat_grad = d_grid.reshape(-1, D)
-    g_emb_w = matmul(active.reshape(-1, channels).T, flat_grad)
     g_emb_b = jnp.sum(flat_grad.astype(full_type), 0)
     d_active = (
         matmul(flat_grad, embed_weight.T)
@@ -228,92 +509,59 @@
             window = widened[:, shift_r : shift_r + rows, shift_c : shift_c + GRID, :].reshape(
                 -1, channels
             )
-            windows.append(matmul(window.T, flat_feat))
-    g_stand = jnp.concatenate(windows, 0)
-    g_conv = wscale * (
-        g_stand - jnp.mean(g_stand, 0) - stand_full * jnp.mean(g_stand * stand_full, 0)
-    )
+            windows.append(window)
+    windows = jnp.concatenate(windows, 1)
     flipped = jnp.flip(kernel, (0, 1)).transpose(0, 1, 3, 2)
     d_rim = padded(d_feat, (("band", 1),), 1)
     image_grad = conv_rows(d_rim, flipped) * row_live
-    shares = (
-        lax.psum_scatter(g_conv, "img", scatter_dimension=0, tiled=True),
-        lax.psum_scatter(g_gn_g, "img", scatter_dimension=0, tiled=True),
-        lax.psum_scatter(g_gn_b, "img", scatter_dimension=0, tiled=True),
-        lax.psum_scatter(g_emb_w, "img", scatter_dimension=0, tiled=True),
-        lax.psum_scatter(g_emb_b, "img", scatter_dimension=0, tiled=True),
-        lax.psum_scatter(g_ln1_g, "img", scatter_dimension=0, tiled=True),
-        lax.psum_scatter(g_ln1_b, "img", scatter_dimension=0, tiled=True),
-        lax.psum_scatter(g_qkv_w, "img", scatter_dimension=0, tiled=True),
-        lax.psum_scatter(g_q_b, "img", scatter_dimension=0, tiled=True),
-        lax.psum_scatter(g_v_b, "img", scatter_dimension=0, tiled=True),
-        lax.psum_scatter(g_out_w, "img", scatter_dimension=1, tiled=True),
-        lax.psum_scatter(g_out_b, "img", scatter_dimension=0, tiled=True),
-        lax.psum_scatter(g_ln2_g, "img", scatter_dimension=0, tiled=True),
-        lax.psum_scatter(g_ln2_b, "img", scatter_dimension=0, tiled=True),
-        lax.psum_scatter(g_up_w, "img", scatter_dimension=0, tiled=True),
-        lax.psum_scatter(g_up_b, "img", scatter_dimension=0, tiled=True),
-        lax.psum_scatter(g_down_w, "img", scatter_dimension=1, tiled=True),
-        lax.psum_scatter(g_down_b, "img", scatter_dimension=0, tiled=True),
-    )
-    s_conv, s_emb, s_qkv, s_out, s_up, s_down = (
-        lax.psum_scatter(shares[0], "band", scatter_dimension=1, tiled=True),
-        lax.psum_scatter(shares[3], "band", scatter_dimension=1, tiled=True),
-        lax.psum_scatter(shares[7], "band", scatter_dimension=1, tiled=True),
-        lax.psum_scatter(shares[10], "band", scatter_dimension=0, tiled=True),
-        lax.psum_scatter(shares[14], "band", scatter_dimension=1, tiled=True),
-        lax.psum_scatter(shares[16], "band", scatter_dimension=0, tiled=True),
-    )
-    vectors = (
-        shares[1],
-        shares[2],
-        shares[4],
-        shares[5],
-        shares[6],
-        shares[8],
-        shares[9],
-        shares[11],
-        shares[12],
-        shares[13],
-        shares[15],
-        shares[17],
-    )
-    vsum = lax.psum(
-        (
-            vectors[0],
-            vectors[1],
-            vectors[2],
-            vectors[3],
-            vectors[4],
-            vectors[5],
-            vectors[6],
-            vectors[7],
-            vectors[8],
-            vectors[9],
-            vectors[10],
-            vectors[11],
-        ),
-        "band",
-    )
+    def tall(v):
+        return jnp.pad(v, ((0, TOK - v.shape[0]), (0, 0)))
+
+    def banded(v, width):
+        v = tall(v).reshape(TOK, 4, -1).transpose(1, 0, 2)
+        return jnp.pad(v, ((0, 0), (0, 0), (0, width - v.shape[2])))
+
+    stats = jnp.mean(windows.astype(full_type), 1)
+    vectors = [g_gn_g, g_gn_b, g_emb_b, g_ln1_g, g_ln1_b, g_q_b, g_v_b, g_out_b, g_ln2_g, g_ln2_b, g_up_b, g_down_b]
+    row_mean = jnp.sum(stats[:, None] * flat_feat.astype(full_type), 0)
+    row_dot = jnp.sum(feat.reshape(-1, channels) * flat_feat.astype(full_type), 0) / conv_weight.shape[0]
+    vec = jnp.concatenate(vectors + [row_mean, row_dot])
+    vec = jnp.pad(vec, (0, -vec.shape[0] % 1024)).reshape(-1, 128)
+    r_down, r_up, r_out, r_qkv, r_conv, r_emb, r_vec = reduce_grads(
+        tall(grad_out), banded(act, D), tall(hidden2), banded(d_pre, D), tall(d_attn), banded(mixed, 256), tall(hidden),
+        banded(d_qkv, 640), tall(windows), tall(flat_feat), tall(active.reshape(-1, channels)), tall(flat_grad), vec)
+    img, band = lax.axis_index("img"), lax.axis_index("band")
+    n_img, n_band = lax.axis_size("img"), lax.axis_size("band")
+    flat = r_vec.reshape(-1)
+    offset = 0
+    vsum = []
+    for v in vectors:
+        size = v.shape[0] // n_img
+        vsum.append(lax.dynamic_slice_in_dim(flat, offset + img * size, size))
+        offset += v.shape[0]
+    m_one, m_two = flat[offset : offset + channels], flat[offset + channels : offset + 2 * channels]
+
+    def own(v, total):
+        size = total // n_img
+        return lax.dynamic_slice_in_dim(v, lax.rem(img, v.shape[0] // size) * size, size)
+
+    def own_band(v, width):
+        return lax.dynamic_slice_in_dim(v, lax.div(band, 2) * width, width, axis=1)
+
+    cols = channels // n_band
+    conv_rows_here = conv_weight.shape[0] // n_img
+    g_conv = own_band(own(r_conv, conv_weight.shape[0]), cols)
+    sl = lambda v: lax.dynamic_slice_in_dim(v, band * cols, cols)
+    own_stand = lax.dynamic_slice(stand_full, (img * conv_rows_here, band * cols), (conv_rows_here, cols))
+    s_conv = sl(wscale) * (g_conv - sl(m_one) - own_stand * sl(m_two))
+    s_emb = own_band(own(r_emb, channels), D // n_band)
+    s_qkv = own(r_qkv, D)[:, : 3 * D // n_band]
+    s_out = own(r_out, D)[:, : D // n_band].T
+    s_up = own(r_up, D)
+    s_down = own(r_down, D).T
     summed = (
-        s_conv,
-        vsum[0],
-        vsum[1],
-        s_emb,
-        vsum[2],
-        vsum[3],
-        vsum[4],
-        s_qkv,
-        vsum[5],
-        vsum[6],
-        s_out,
-        vsum[7],
-        vsum[8],
-        vsum[9],
-        s_up,
-        vsum[10],
-        s_down,
-        vsum[11],
+        s_conv, vsum[0], vsum[1], s_emb, vsum[2], vsum[3], vsum[4], s_qkv, vsum[5], vsum[6], s_out, vsum[7], vsum[8], vsum[9],
+        s_up, vsum[10], s_down, vsum[11],
     )
     return (encoded, image_grad, text_grad) + summed
 

time: 970 us -> 401 us (0.41)
  the two profiles are of different devices: /device:TPU:0 before, /device:TPU:9 now
where the time goes in v1:
time: 401 us; the launch traced here: 394 us
  local copies, waits for them, and re-layouts  166 us (41%)
  Pallas kernels  110 us (27%)
  other arithmetic  40.9 us (10%)
  matrix products  39.4 us (10%)
  starting transfers between devices  22.7 us (6%)
  blocking collectives  12.1 us (3%)
    pallas_call x1, Pallas kernels, reduce_grads(): pl.pallas_call(functools.partial(grads_kernel, plans, vec.shape[0]), out_...  110 us
    unnamed x162, local copies, waits for them, and re-layouts  44.8 us
    dot_general x10, matrix products, matmul(): return jnp.dot(left, right, preferred_element_type=jnp.float32)  27.9 us
    pad x12, local copies, waits for them, and re-layouts, tall(): return jnp.pad(v, ((0, TOK - v.shape[0]), (0, 0)))  22.2 us
    reshape x9, local copies, waits for them, and re-layouts, body(): widened[:, shift_r:shift_r + rows, shift_c:shift_c + GRID, :]  14.3 us
    slice x9, local copies, waits for them, and re-layouts, body(): widened[:, shift_r:shift_r + rows, shift_c:shift_c + GRID, :]  11.7 us
    reshape x4, local copies, waits for them, and re-layouts, banded(): v = tall(v).reshape(TOK, 4, -1).transpose(1, 0, 2)  9.63 us
    ppermute x2, starting transfers between devices, padded(): lax.ppermute(tail, axis, [(i, (i + 1) % count) for i in range(ends)])  9.3 us
  transfers between devices with their start and end apart: 6, of which 0 were waited for; matrix products, arithmetic and copies ran while one was open for 25% of the time, Pallas kernels for 0%

profile of v1, /device:TPU:9, one launch (start us, length us, event | category | flops | bytes accessed | tf_op | source)
XLA Modules:
  0.0 393.7 jit_solution(16984701725890359422)
XLA Ops:
  3.2 3.7 collective-permute-start
  6.9 1.9 collective-permute-start.1
  12.1 2.1 fusion.6
  20.8 2.7 fusion.64
  26.8 6.1 %all-reduce.18 = (f32[4,32]{1,0:T(4,128)}, f32[4,32]{1,0:T(4,128)}) all-reduce(f32[4,32]{1,0:T(4,128)S(1)} %reduce_sum.314, f32[4,32]{1,0:T(4,128)S(1)} %reduce_sum.311), channel_id=1, replica_groups=mesh['img'=8,'band'=4] {'band'}, use_global_device_ids=true, to_apply=%region_7.0 | all-reduce | flops 256 | bytes 2048 | tf_op jit(solution)/shard_map/psum | solution.py:400
  37.0 2.7 multiply_convert_fusion.3
  42.0 2.0 fusion.24
  44.0 1.8 reshape.375
  45.8 1.9 copy.140
  47.7 5.5 %all-to-all-start = ((bf16[4,4,14,768]{3,1,2,0:T(4,128)(2,1)}), bf16[4,4,14,768]{3,1,2,0:T(4,128)(2,1)}, u32[]{:S(2)}, u32[]{:S(2)}) async-start(bf16[4,4,14,768]{3,1,2,0:T(4,128)(2,1)} %copy.140), calls=%async_computation | async-start | bytes 688128 | tf_op jit(solution)/shard_map/all_to_all | solution.py:411
  96.7 2.4 pad.74.refs_8_
  101.2 1.8 copy.141
  103.0 1.8 all_to_all.7
  104.8 1.8 copy.142
  106.6 1.8 convert_element_type.168
  115.5 1.9 copy.144
  117.4 1.9 copy.145
  119.3 1.9 copy.143
  121.2 1.9 fusion.71
  127.5 8.3 %multiply_convert_fusion.1 = (bf16[228,3072]{1,0:T(8,128)(2,1)}, f32[228,3072]{1,0:T(8,128)S(1)}, f32[228,3072]{1,0:T(8,128)S(1)}) fusion(f32[3072]{0:T(1024)S(1)} %copy-done.59, bf16[228,768]{1,0:T(8,128)(2,1)S(1)} %add_convert_fusion.1, bf16[768,3072]{1,0:T(8,128)(2,1)S(1)} %bitcast.180), kind=kOutput, calls=%fused_computation.10 | convolution fusion | flops 1122066432 | bytes 12085248 | tf_op jit(solution)/shard_map/dot_general | solution.py:319
  135.9 2.7 convert_reduce_fusion.1
  138.6 2.3 multiply_reduce_fusion.1
  140.9 1.8 convert_reduce_fusion.8
  144.7 1.9 copy.147
  146.6 3.0 multiply_reduce_fusion
  152.2 2.7 fusion.43
  156.1 2.6 copy.180
  158.8 1.9 pad.67.refs_4_
  162.4 1.8 pad.68
  171.4 4.1 %all-to-all-start.1 = ((bf16[1,16,14,768]{3,2,0,1:T(8,128)(2,1)}), bf16[1,16,14,768]{3,2,0,1:T(8,128)(2,1)}, u32[]{:S(2)}, u32[]{:S(2)}) async-start(bf16[1,16,14,768]{3,2,0,1:T(8,128)(2,1)} %pad.62), calls=%async_computation.1 | async-start | bytes 786432 | tf_op jit(solution)/shard_map/all_to_all | solution.py:483
  175.5 2.5 pad.71
  178.0 2.4 copy.161
  180.4 2.6 pad.72.refs_7_
  184.5 2.6 copy.159
  187.1 2.6 copy.179
  189.7 2.8 pad.64.clone
  192.5 2.6 copy.157
  195.1 2.0 copy.160
  197.1 1.9 pad.69.refs_5_
  199.1 5.0 %fusion.25 = bf16[1,228,768]{2,1,0:T(8,128)(2,1)} fusion(f32[228,768]{1,0:T(8,128)} %copy-done.7, bf16[228,3072]{1,0:T(8,128)(2,1)} %get-tuple-element.144, bf16[3072,768]{1,0:T(8,128)(2,1)} %param.39, f32[768]{0:T(1024)S(1)} %copy-done.61), kind=kOutput, calls=%fused_computation.50 | convolution fusion | flops 1076364288 | bytes 7173120 | tf_op jit(solution)/shard_map/dot_general | solution.py:319
  205.7 1.9 reshape.389
  207.5 2.1 fusion.27
  213.1 2.9 multiply_reduce_fusion.6
  219.3 6.0 %all-reduce.17 = (f32[4,32]{1,0:T(4,128)}, f32[4,32]{1,0:T(4,128)}) all-reduce(f32[4,32]{1,0:T(4,128)S(1)} %reduce_sum.330, f32[4,32]{1,0:T(4,128)S(1)} %reduce_sum.327), channel_id=1, replica_groups=mesh['img'=8,'band'=4] {'band'}, use_global_device_ids=true, to_apply=%region_24.25 | all-reduce | flops 256 | bytes 2048 | tf_op jit(solution)/shard_map/psum | solution.py:497
  256.5 110.1 %shard_map.373 = (f32[96,768]{1,0:T(8,128)}, f32[96,768]{1,0:T(8,128)}, f32[96,256]{1,0:T(8,128)}, f32[96,640]{1,0:T(8,128)}, f32[288,128]{1,0:T(8,128)}, /*index=5*/f32[32,384]{1,0:T(8,128)}, f32[88,128]{1,0:T(8,128)}) custom-call(bf16[256,768]{1,0:T(8,128)(2,1)} %pad.63.refs_0_, bf16[4,256,768]{2,1,0:T(8,128)(2,1)} %bitcast.143, ...), custom_call_target="tpu_custom_call" | custom-call | tf_op jit(solution)/shard_map/pallas_call | solution.py:291
  369.0 5.6 %collective-permute-start.2 = (bf16[4,1,14,256]{3,0,2,1:T(4,128)(2,1)}, bf16[4,1,14,256]{3,0,2,1:T(4,128)(2,1)}, u32[]{:S(2)}, u32[]{:S(2)}) collective-permute-start(bf16[4,1,14,256]{3,0,2,1:T(4,128)(2,1)} %get-tuple-element.159), channel_id=1, source_target_pairs={{0,1},{1,2},{2,3},{4,5},{5,6},{6,7},{8,9},{9,10},{10,11},{12,13},{... | collective-permute-start | bytes 86024 | tf_op jit(solution)/shard_map/ppermute | solution.py:309
  374.6 1.9 collective-permute-start.3
  378.0 1.8 subtract_multiply_fusion.2
  (288 shorter events, 151.1 us)
Async XLA Ops:
  0.7 112.0 %copy-start = (bf16[768,2304]{1,0:T(8,128)(2,1)S(1)}, bf16[768,2304]{1,0:T(8,128)(2,1)}, u32[]{:S(2)}) copy-start(bf16[768,2304]{1,0:T(8,128)(2,1)} %param.30) | copy-start | bytes 10616836
  0.7 11.4 %copy-start.3 = (bf16[2304,256]{1,0:T(8,128)(2,1)S(1)}, bf16[2304,256]{1,0:T(8,128)(2,1)}, u32[]{:S(2)}) copy-start(bf16[2304,256]{1,0:T(8,128)(2,1)} %param.23) | copy-start | bytes 3538948
  3.2 17.6 %collective-permute-start = (bf16[4,1,14,256]{3,0,2,1:T(4,128)(2,1)}, bf16[4,1,14,256]{3,0,2,1:T(4,128)(2,1)}, u32[]{:S(2)}, u32[]{:S(2)}) collective-permute-start(bf16[4,1,14,256]{3,0,2,1:T(4,128)(2,1)} %get-tuple-element.163), channel_id=1, source_target_pairs={{0,1},{1,2},{2,3},{4,5},{5,6},{6,7},{8,9},{9,10},{10,11},{12,13},{... | collective-permute-start | bytes 86024 | tf_op jit(solution)/shard_map/ppermute | solution.py:309
  6.9 13.9 %collective-permute-start.1 = (bf16[4,1,14,256]{3,0,2,1:T(4,128)(2,1)}, bf16[4,1,14,256]{3,0,2,1:T(4,128)(2,1)}, u32[]{:S(2)}, u32[]{:S(2)}) collective-permute-start(bf16[4,1,14,256]{3,0,2,1:T(4,128)(2,1)} %get-tuple-element.164), channel_id=1, source_target_pairs={{1,0},{2,1},{3,2},{5,4},{6,5},{7,6},{9,8},{10,9},{11,10},{13,12},{... | collective-permute-start | bytes 86024 | tf_op jit(solution)/shard_map/ppermute | solution.py:311
  8.8 28.1 %copy-start.50 = (f32[4]{0:T(128)}, f32[4]{0:T(128)S(1)}, u32[]{:S(2)}) copy-start(f32[4]{0:T(128)S(1)} %compare_convert_fusion) | copy-start | bytes 52
  14.1 22.8 %copy-start.49 = (f32[256]{0:T(256)S(1)}, f32[256]{0:T(256)}, u32[]{:S(2)}) copy-start(f32[256]{0:T(256)} %param.24) | copy-start | bytes 3076
  35.3 22.1 %copy-start.35 = (f32[4,256]{1,0:T(4,128)}, f32[4,256]{1,0:T(4,128)S(1)}, u32[]{:S(2)}) copy-start(f32[4,256]{1,0:T(4,128)S(1)} %mul.378) | copy-start | bytes 12292
  37.0 20.5 %copy-start.37 = (f32[4,256]{1,0:T(4,128)}, f32[4,256]{1,0:T(4,128)S(1)}, u32[]{:S(2)}) copy-start(f32[4,256]{1,0:T(4,128)S(1)} %sub.123) | copy-start | bytes 12292
  47.7 53.5 %all-to-all-start = ((bf16[4,4,14,768]{3,1,2,0:T(4,128)(2,1)}), bf16[4,4,14,768]{3,1,2,0:T(4,128)(2,1)}, u32[]{:S(2)}, u32[]{:S(2)}) async-start(bf16[4,4,14,768]{3,1,2,0:T(4,128)(2,1)} %copy.140), calls=%async_computation | async-start | bytes 688128 | tf_op jit(solution)/shard_map/all_to_all | solution.py:411
  82.0 14.1 %copy-start.26 = (bf16[224,256]{1,0:T(8,128)(2,1)S(1)}, bf16[224,256]{1,0:T(8,128)(2,1)}, u32[]{:S(2)}) copy-start(bf16[224,256]{1,0:T(8,128)(2,1)} %reshape.374) | copy-start | bytes 344068
  96.7 14.7 %copy-start.43 = (f32[768]{0:T(1024)S(1)}, f32[768]{0:T(1024)}, u32[]{:S(2)}) copy-start(f32[768]{0:T(1024)} %param.28) | copy-start | bytes 9220
  96.7 14.7 %copy-start.52 = (f32[768]{0:T(1024)S(1)}, f32[768]{0:T(1024)}, u32[]{:S(2)}) copy-start(f32[768]{0:T(1024)} %param.29) | copy-start | bytes 9220
  113.7 7.5 %copy-start.58 = (pred[228]{0:T(512)(128)(4,1)S(1)}, pred[228]{0:T(512)(128)(4,1)}, u32[]{:S(2)}) copy-start(pred[228]{0:T(512)(128)(4,1)} %iota_compare_fusion.1) | copy-start | bytes 688
  123.1 4.3 %slice-start = ((s8[4718592]{0:T(1024)(128)(4,1)}), s8[4194304]{0:T(1024)(128)(4,1)S(1)}, s32[]{:S(2)}) async-start(s8[4718592]{0:T(1024)(128)(4,1)} %bitcast.179), calls=%async_computation.2 | async-start | bytes 8388608
  123.6 2.8 copy-start.25
  123.6 2.8 copy-start.27
  123.7 3.8 slice-start.1
  124.7 2.8 copy-start.59
  127.0 13.9 %copy-start.7 = (f32[228,768]{1,0:T(8,128)}, f32[228,768]{1,0:T(8,128)S(1)}, u32[]{:S(2)}) copy-start(f32[228,768]{1,0:T(8,128)S(1)} %get-tuple-element.184) | copy-start | bytes 2101252
  127.0 8.9 %slice-start.2 = ((s8[4718592]{0:T(1024)(128)(4,1)}), s8[4194304]{0:T(1024)(128)(4,1)S(1)}, s32[]{:S(2)}) async-start(s8[4718592]{0:T(1024)(128)(4,1)} %bitcast.181), calls=%async_computation.4 | async-start | bytes 8388608
  127.5 8.4 %copy-start.22 = (bf16[228,768]{1,0:T(8,128)(2,1)}, bf16[228,768]{1,0:T(8,128)(2,1)S(1)}, u32[]{:S(2)}) copy-start(bf16[228,768]{1,0:T(8,128)(2,1)S(1)} %add_convert_fusion.1) | copy-start | bytes 1050628
  127.5 8.4 %copy-start.23 = (bf16[1,228,768]{2,1,0:T(8,128)(2,1)S(1)}, bf16[1,228,768]{2,1,0:T(8,128)(2,1)}, u32[]{:S(2)}) copy-start(bf16[1,228,768]{2,1,0:T(8,128)(2,1)} %param.43) | copy-start | bytes 1050628
  127.5 8.4 %slice-start.3 = ((s8[4718592]{0:T(1024)(128)(4,1)}), s8[524288]{0:T(1024)(128)(4,1)S(1)}, s32[]{:S(2)}) async-start(s8[4718592]{0:T(1024)(128)(4,1)} %bitcast.181), calls=%async_computation.5 | async-start | bytes 1048576
  146.6 3.0 copy-start.2
  150.9 4.0 %copy-start.12 = (bf16[12,64,228]{2,1,0:T(8,128)(2,1)}, bf16[12,64,228]{2,1,0:T(8,128)(2,1)S(1)}, u32[]{:S(2)}) copy-start(bf16[12,64,228]{2,1,0:T(8,128)(2,1)S(1)} %fusion.16) | copy-start | bytes 1050628
  152.1 2.8 copy-start.9
  156.1 9.9 %copy-start.41 = (f32[228]{0:T(256)S(1)}, f32[228]{0:T(256)}, u32[]{:S(2)}) copy-start(f32[228]{0:T(256)} %copy-done.39) | copy-start | bytes 2740
  156.1 9.9 %copy-start.45 = (f32[768]{0:T(1024)S(1)}, f32[768]{0:T(1024)}, u32[]{:S(2)}) copy-start(f32[768]{0:T(1024)} %param.28) | copy-start | bytes 9220
  156.1 9.9 %copy-start.48 = (f32[228]{0:T(256)S(1)}, f32[228]{0:T(256)}, u32[]{:S(2)}) copy-start(f32[228]{0:T(256)} %copy-done.46) | copy-start | bytes 2740
  158.8 7.2 %copy-start.56 = (f32[228]{0:T(256)S(1)}, f32[228]{0:T(256)}, u32[]{:S(2)}) copy-start(f32[228]{0:T(256)} %get-tuple-element.122) | copy-start | bytes 2740
  158.8 7.3 %copy-start.6 = (bf16[1,196,768]{2,1,0:T(8,128)(2,1)S(1)}, bf16[1,196,768]{2,1,0:T(8,128)(2,1)}, u32[]{:S(2)}) copy-start(bf16[1,196,768]{2,1,0:T(8,128)(2,1)} %convert_element_type.168) | copy-start | bytes 903172
  158.8 7.3 %copy-start.18 = (f32[228,768]{1,0:T(8,128)S(1)}, f32[228,768]{1,0:T(8,128)}, u32[]{:S(2)}) copy-start(f32[228,768]{1,0:T(8,128)} %get-tuple-element.142) | copy-start | bytes 2101252
  158.8 7.3 %copy-start.29 = (bf16[1,32,768]{2,1,0:T(8,128)(2,1)S(1)}, bf16[1,32,768]{2,1,0:T(8,128)(2,1)}, u32[]{:S(2)}) copy-start(bf16[1,32,768]{2,1,0:T(8,128)(2,1)} %param.41) | copy-start | bytes 147460
  158.8 7.3 %copy-start.30 = (f32[228,768]{1,0:T(8,128)S(1)}, f32[228,768]{1,0:T(8,128)}, u32[]{:S(2)}) copy-start(f32[228,768]{1,0:T(8,128)} %get-tuple-element.189) | copy-start | bytes 2101252
  171.4 34.3 %all-to-all-start.1 = ((bf16[1,16,14,768]{3,2,0,1:T(8,128)(2,1)}), bf16[1,16,14,768]{3,2,0,1:T(8,128)(2,1)}, u32[]{:S(2)}, u32[]{:S(2)}) async-start(bf16[1,16,14,768]{3,2,0,1:T(8,128)(2,1)} %pad.62), calls=%async_computation.1 | async-start | bytes 786432 | tf_op jit(solution)/shard_map/all_to_all | solution.py:483
  192.5 6.6 %copy-start.61 = (f32[768]{0:T(1024)S(1)}, f32[768]{0:T(1024)}, u32[]{:S(2)}) copy-start(f32[768]{0:T(1024)} %param.40) | copy-start | bytes 9220
  199.1 5.0 %copy-start.13 = (bf16[12,64,228]{2,1,0:T(8,128)(2,1)S(1)}, bf16[12,64,228]{2,1,0:T(8,128)(2,1)}, u32[]{:S(2)}) copy-start(bf16[12,64,228]{2,1,0:T(8,128)(2,1)} %copy-done.12) | copy-start | bytes 1050628
  199.1 5.8 %copy-start.10 = (bf16[12,64,228]{2,1,0:T(8,128)(2,1)S(1)}, bf16[12,64,228]{2,1,0:T(8,128)(2,1)}, u32[]{:S(2)}) copy-start(bf16[12,64,228]{2,1,0:T(8,128)(2,1)} %copy-done.9) | copy-start | bytes 1050628
  204.1 9.0 %copy-start.36 = (f32[4,256]{1,0:T(4,128)S(1)}, f32[4,256]{1,0:T(4,128)}, u32[]{:S(2)}) copy-start(f32[4,256]{1,0:T(4,128)} %copy-done.35) | copy-start | bytes 12292
  204.1 9.0 %copy-start.38 = (f32[4,256]{1,0:T(4,128)S(1)}, f32[4,256]{1,0:T(4,128)}, u32[]{:S(2)}) copy-start(f32[4,256]{1,0:T(4,128)} %copy-done.37) | copy-start | bytes 12292
  256.5 121.6 %copy-start.57 = (f32[64]{0:T(128)S(1)}, f32[64]{0:T(128)}, u32[]{:S(2)}) copy-start(f32[64]{0:T(128)} %dynamic_slice.60) | copy-start | bytes 772
  366.5 22.2 %copy-start.51 = (f32[4]{0:T(128)S(1)}, f32[4]{0:T(128)}, u32[]{:S(2)}) copy-start(f32[4]{0:T(128)} %copy-done.50) | copy-start | bytes 52
  366.5 22.2 %copy-start.62 = (pred[32,2]{0,1:T(4,128)(4,1)S(1)}, pred[32,2]{0,1:T(4,128)(4,1)}, u32[]{:S(2)}) copy-start(pred[32,2]{0,1:T(4,128)(4,1)} %constant.260) | copy-start | bytes 196
  369.0 18.3 %collective-permute-start.2 = (bf16[4,1,14,256]{3,0,2,1:T(4,128)(2,1)}, bf16[4,1,14,256]{3,0,2,1:T(4,128)(2,1)}, u32[]{:S(2)}, u32[]{:S(2)}) collective-permute-start(bf16[4,1,14,256]{3,0,2,1:T(4,128)(2,1)} %get-tuple-element.159), channel_id=1, source_target_pairs={{0,1},{1,2},{2,3},{4,5},{5,6},{6,7},{8,9},{9,10},{10,11},{12,13},{... | collective-permute-start | bytes 86024 | tf_op jit(solution)/shard_map/ppermute | solution.py:309
  374.6 12.7 %collective-permute-start.3 = (bf16[4,1,14,256]{3,0,2,1:T(4,128)(2,1)}, bf16[4,1,14,256]{3,0,2,1:T(4,128)(2,1)}, u32[]{:S(2)}, u32[]{:S(2)}) collective-permute-start(bf16[4,1,14,256]{3,0,2,1:T(4,128)(2,1)} %get-tuple-element.160), channel_id=1, source_target_pairs={{1,0},{2,1},{3,2},{5,4},{6,5},{7,6},{9,8},{10,9},{11,10},{13,12},{... | collective-permute-start | bytes 86024 | tf_op jit(solution)/shard_map/ppermute | solution.py:311
  385.9 5.5 %copy-start.34 = (f32[96,640]{1,0:T(8,128)S(1)}, f32[96,640]{1,0:T(8,128)}, u32[]{:S(2)}) copy-start(f32[96,640]{1,0:T(8,128)} %get-tuple-element.31) | copy-start | bytes 737284
  388.3 3.7 copy-start.33
  388.5 4.3 %copy-start.32 = (f32[96,768]{1,0:T(8,128)S(1)}, f32[96,768]{1,0:T(8,128)}, u32[]{:S(2)}) copy-start(f32[96,768]{1,0:T(8,128)} %get-tuple-element.34) | copy-start | bytes 884740
  (25 other events, 39.7 us)

commit v2 on v0

v2 whole, which is shorter than its diff:
```python
import functools
import types

import jax
import jax.numpy as jnp
from jax import lax
from jax.experimental import pallas as pl
from jax.experimental.pallas import tpu as pltpu
from jax.sharding import PartitionSpec as P

D = 768
FF = 3072
HEADS = 12
GROUPS = 32
GRID = 14
TEXT = 32
PATCHES = 196
WIDE = 16
TOK = 256
CELLS = GRID * WIDE
HALF = jnp.bfloat16
FULL = jnp.float32
MESH_ID = pl.DeviceIdType.MESH
CORE = ("band", 1)
FAR = ("band", 2)


def bit_of(value, bit):
    return lax.rem(lax.div(value, bit), 2)


def flip(value, bit):
    return value + bit * (1 - 2 * bit_of(value, bit))


def partner(label):
    axis, bit = label
    img, band = lax.axis_index("img"), lax.axis_index("band")
    return (flip(img, bit), band) if axis == "img" else (img, flip(band, bit))


def my_bit(label):
    axis, bit = label
    return bit_of(lax.axis_index(axis), bit)


def bits(count):
    return [1 << k for k in range(count.bit_length() - 1)]


class Plan:
    def __init__(self, n_img, rows, width, lead, order):
        self.width = width
        split = [("img", k) for k in reversed(bits(n_img)) if (rows // n_img) * k % 16 == 0]
        self.rows = rows >> len(split)
        self.first = ([lead] if lead else []) + split
        rest = [("img", k) for k in bits(n_img) if ("img", k) not in split]
        ordered = [lab for lab in order if lab in self.first]
        self.order = ordered + rest + [lab for lab in order if lab not in self.first and lab[0] == "band"]
        self.shapes = []
        labels = list(self.first)
        for lab in self.order:
            if lab in labels:
                labels.remove(lab)
            self.shapes.append((2,) * len(labels) + (self.rows, width))
        self.shape = (2,) * len(self.first) + (self.rows, width)

    def scratch(self):
        return [self.shape] + self.shapes


class Piece:
    def __init__(self, plan, refs, sems, slot, out, at):
        self.plan, self.buf, self.recv = plan, refs[0], refs[1:]
        self.sems, self.slot = sems, slot
        self.labels, self.cur = list(plan.first), refs[0]
        self.sent = []
        self.out = out.at[:, pl.ds(at, plan.width)]
        self.stage = 0

    def _index(self, label, which):
        at = self.labels.index(label)
        return (slice(None),) * at + (which,)

    def start(self):
        label = self.plan.order[self.stage]
        src = self.cur
        if label in self.labels:
            src = src.at[self._index(label, 1 - my_bit(label))]
        send, recv = self.sems
        copy = pltpu.make_async_remote_copy(
            src_ref=src,
            dst_ref=self.recv[self.stage],
            send_sem=send.at[self.slot + self.stage],
            recv_sem=recv.at[self.slot + self.stage],
            device_id=partner(label),
            device_id_type=MESH_ID,
        )
        copy.start()
        self.sent.append(copy)

    def step(self):
        label = self.plan.order[self.stage]
        self.sent[self.stage].wait_recv()
        mine = self.cur
        if label in self.labels:
            mine = mine[self._index(label, my_bit(label))]
            self.labels.remove(label)
        else:
            mine = mine[...]
        got = self.recv[self.stage]
        self.stage += 1
        if self.stage == len(self.plan.order):
            self.out[...] = (got[...].astype(FULL) + mine.astype(FULL)).reshape(self.out.shape)
        else:
            got[...] = got[...] + mine
            self.cur = got
            self.start()

    def drain(self):
        for copy in self.sent:
            copy.wait_send()


def dot(left, right):
    return jnp.dot(left, right, preferred_element_type=FULL)


def dot_tn(left, right):
    return lax.dot_general(left, right, (((0,), (0,)), ((), ())), preferred_element_type=FULL)


def dot_nt(left, right):
    return lax.dot_general(left, right, (((1,), (1,)), ((), ())), preferred_element_type=FULL)


def exact_dot(left, right):
    return jnp.dot(left, right, precision=lax.Precision.HIGHEST, preferred_element_type=FULL)


def gelu_parts(x):
    cdf = 0.5 + 0.5 * lax.erf(x * 0.7071067811865476)
    pdf = jnp.exp(-0.5 * x * x) * 0.3989422804014327
    return x * cdf, cdf + x * pdf


def iota(shape, axis):
    return lax.broadcasted_iota(jnp.int32, shape, axis)


def row(ref):
    return ref[...].reshape(1, -1)


def column_sum(values):
    return jnp.sum(values, 0, keepdims=True)


def shifted(values):
    edge = jnp.zeros(values.shape[:2] + (1, values.shape[3]), FULL)
    left = jnp.concatenate([edge, values[:, :, : WIDE - 1]], 2)
    right = jnp.concatenate([values[:, :, 1:], edge], 2)
    return left, values, right


def layer_kernel(names, plans, *refs):
    r = types.SimpleNamespace(**dict(zip(names, refs)))
    img, band = lax.axis_index("img"), lax.axis_index("band")
    n_img, n_band = lax.axis_size("img"), lax.axis_size("band")
    images, rows = r.image.shape[:2]
    channels = r.conv_weight.shape[1]
    core = my_bit(CORE)
    others = [lax.rem(band + d, n_band) for d in range(n_band)]

    fetches = {}

    def fetch(name, at):
        copy = pltpu.make_async_copy(getattr(r, name), getattr(r, "v_" + name), r.fetch_sem.at[at])
        copy.start()
        fetches[name] = copy

    for at, name in enumerate(("conv_weight", "embed_weight", "qkv_weight", "cotangent", "text_embed", "out_weight", "up_weight", "down_weight")):
        fetch(name, at)

    links = [CORE, FAR] + [("img", k) for k in bits(n_img)]
    barrier = pltpu.get_barrier_semaphore()
    for d in range(1, n_band):
        pl.semaphore_signal(barrier, inc=1, device_id=(img, others[d]), device_id_type=MESH_ID)
    for label in links[2:]:
        pl.semaphore_signal(barrier, inc=1, device_id=partner(label), device_id_type=MESH_ID)
    pl.semaphore_wait(barrier, n_band - 1 + len(links) - 2)

    pending = []

    def send(src, dst, at, device):
        copy = pltpu.make_async_remote_copy(
            src_ref=src, dst_ref=dst, send_sem=r.send_sem.at[at], recv_sem=r.recv_sem.at[at],
            device_id=device, device_id_type=MESH_ID)
        copy.start()
        pending.append(copy)
        return copy

    def edge_rows(ref, at):
        up = send(ref.at[:, rows], ref.at[:, 0], at, (img, others[1]))
        down = send(ref.at[:, 1], ref.at[:, rows + 1], at + 1, (img, others[n_band - 1]))
        return up, down

    def edges_in(ref, copies):
        for copy in copies:
            copy.wait_recv()
        values = ref[...].astype(FULL)
        at = iota(values.shape, 1) + band * rows
        return jnp.where((at == 0) | (at > n_band * rows), 0.0, values)

    def exchange(values, slots, at):
        slots[0] = values
        copies = [send(slots.at[0], slots.at[d], at + d - 1, (img, others[d])) for d in range(1, n_band)]
        for d, copy in enumerate(copies, 1):
            copy.wait_recv()
            values = values + slots[d]
        return values

    def to_owners(src, dst, at):
        copies = [send(src.at[others[d]], dst.at[band], at + d - 1, (img, others[d])) for d in range(1, n_band)]
        dst[band] = src[band]
        for copy in copies:
            copy.wait_recv()

    r.pixels[:, 1 : rows + 1, GRID:, :] = jnp.zeros((images, rows, WIDE - GRID, channels), HALF)
    at_row = iota((images, rows, GRID, channels), 1) + band * rows
    r.pixels[:, 1 : rows + 1, :GRID, :] = jnp.where(at_row < GRID, r.image[...].astype(FULL), 0.0).astype(HALF)
    copies = edge_rows(r.pixels, 0)

    fetches["conv_weight"].wait()
    taps = r.conv_weight.shape[0]
    chunks = [slice(k, k + 256) for k in range(0, taps, 256)]
    wmean = sum(column_sum(r.v_conv_weight[s].astype(FULL)) for s in chunks) * (1.0 / taps)
    wvar = 0.0
    for s in chunks:
        cent = r.v_conv_weight[s].astype(FULL) - wmean
        wvar = wvar + column_sum(cent * cent)
    wscale = lax.rsqrt(wvar * (1.0 / taps) + 1e-05)
    for s in chunks:
        r.v_conv_weight[s] = ((r.v_conv_weight[s].astype(FULL) - wmean) * wscale).astype(HALF)
    r.o_wstat[0:1] = wmean
    r.o_wstat[1:2] = wscale

    pixels = edges_in(r.pixels, copies)
    for e, values in enumerate(shifted(pixels)):
        r.views[e] = values.astype(HALF)

    def window(views, a, e):
        return views[e, :, a : a + rows].reshape(TOK, channels)

    place = iota((TOK, channels), 0)
    live = (lax.rem(place, WIDE) < GRID) & (lax.rem(lax.div(place, WIDE), rows) + band * rows < GRID)
    feat = 0.0
    tap_sum = 0.0
    for a in range(3):
        for e in range(3):
            seen = window(r.views, a, e)
            feat = feat + dot(seen, r.v_conv_weight[(3 * a + e) * channels : (3 * a + e + 1) * channels])
            tap_sum = tap_sum + seen.astype(FULL)
    feat = jnp.where(live, feat, 0.0)
    r.feat[...] = feat
    r.tap_sum[...] = jnp.broadcast_to(jnp.sum(tap_sum, 1, keepdims=True), (TOK, 128))
    per_group = channels // GROUPS
    entries = 1.0 / (GRID * GRID * per_group)
    same = lax.div(iota((channels, channels), 0), per_group) == lax.div(iota((channels, channels), 1), per_group)
    same = jnp.where(same, 1.0, 0.0)
    cells = TOK // images

    def image_sums(one, two):
        one = jnp.sum(one.reshape(images, cells, channels), 1)
        two = jnp.sum(two.reshape(images, cells, channels), 1)
        return exact_dot(jnp.concatenate([one, two], 0), same)

    def per_image(sums, which):
        return sums[which * images : (which + 1) * images].reshape(images, 1, channels)

    sums = exchange(image_sums(feat, feat * feat), r.sums, 2) * entries
    gmean = per_image(sums, 0)
    gscale = lax.rsqrt(per_image(sums, 1) - gmean * gmean + 1e-05)
    zhat = ((feat.reshape(images, cells, channels) - gmean) * gscale).reshape(TOK, channels)
    r.zhat[...] = zhat
    stem, slope = gelu_parts(zhat * row(r.gn_gain) + row(r.gn_bias))
    r.active[...] = jnp.where(live, stem, 0.0).astype(HALF)
    r.slope[...] = jnp.where(live, slope, 0.0)
    fetches["embed_weight"].wait()
    embedded = dot(r.active[...], r.v_embed_weight[...]) + row(r.embed_bias)
    r.embedded[...] = embedded.astype(HALF).reshape(images, cells, D)
    to_owners(r.embedded, r.patches, 5)

    def norm(values):
        mean = jnp.mean(values, -1, keepdims=True)
        cent = values - mean
        rstd = lax.rsqrt(jnp.mean(cent * cent, -1, keepdims=True) + 1e-06)
        return cent * rstd, rstd

    def norm_back(grad, nhat, rstd, gain):
        s = grad * gain
        inner = s - jnp.mean(s, -1, keepdims=True) - nhat * jnp.mean(s * nhat, -1, keepdims=True)
        return inner * rstd

    fetches["text_embed"].wait()
    r.stream[...] = r.patches[...].reshape(TOK, D).astype(FULL)
    r.stream[CELLS:] = r.v_text_embed[0].astype(FULL)
    nhat, rstd_one = norm(r.stream[...])
    r.nhat_one[...] = nhat
    r.rstd_one[...] = rstd_one
    r.hidden[...] = (nhat * row(r.ln1_gain) + row(r.ln1_bias)).astype(HALF)
    fetches["qkv_weight"].wait()
    for k, bias in enumerate((r.query_bias, None, r.value_bias)):
        values = dot(r.hidden[...], r.v_qkv_weight[:, k * D : (k + 1) * D])
        if bias is not None:
            values = values + row(bias)
        values = values.astype(HALF)
        r.qkv[:, k * D : (k + 1) * D] = values * 0.125 if k == 0 else values

    key_at = iota((1, TOK), 1)
    key_live = ((key_at < CELLS) & (lax.rem(key_at, WIDE) < GRID)) | ((key_at >= CELLS) & (key_at - CELLS < r.text_len[0]))
    first = iota((TOK, 128), 1) < 64
    zero = jnp.zeros((TOK, 128), HALF)

    def pair_of(ref, k, p):
        return ref[:, pl.ds(pl.multiple_of(k * D + p * 128, 128), 128)]

    def only(values, h):
        return jnp.where(first, values, zero) if h == 0 else jnp.where(first, zero, values)

    def attend(p, carry):
        query, key, value = (pair_of(r.qkv, k, p) for k in range(3))
        sides = []
        for h in range(2):
            scores = jnp.where(key_live, dot_nt(only(query, h), key), -1000000000.0)
            expd = jnp.exp(scores - jnp.max(scores, -1, keepdims=True))
            probs = expd * (1.0 / jnp.sum(expd, -1, keepdims=True))
            r.probs[2 * p + h] = probs
            sides.append(dot(probs.astype(HALF), value))
        r.mixed[:, pl.ds(pl.multiple_of(p * 128, 128), 128)] = jnp.where(first, *sides).astype(HALF)
        return carry

    lax.fori_loop(0, HEADS // 2, attend, 0)
    fetches["out_weight"].wait()
    mid = r.stream[...] + dot(r.mixed[...], r.v_out_weight[...]) + row(r.out_bias)
    r.final[...] = mid + row(r.down_bias)
    nhat, rstd_two = norm(mid)
    r.nhat_two[...] = nhat
    r.rstd_two[...] = rstd_two
    r.hidden2[...] = (nhat * row(r.ln2_gain) + row(r.ln2_bias)).astype(HALF)

    fetches["cotangent"].wait()
    seq = r.cotangent.shape[1]

    def token_of(at):
        return jnp.where(at < CELLS, jnp.where(lax.rem(at, WIDE) < GRID, lax.div(at, WIDE) * GRID + lax.rem(at, WIDE), -1), at - CELLS + PATCHES)

    spread = jnp.where(token_of(iota((TOK, seq), 0)) == iota((TOK, seq), 1), 1.0, 0.0).astype(HALF)
    gather = jnp.where(token_of(iota((seq, TOK), 1)) == iota((seq, TOK), 0), 1.0, 0.0).astype(HALF)
    r.cot[...] = dot(spread, r.v_cotangent[0]).astype(HALF)

    fetches["up_weight"].wait()
    fetches["down_weight"].wait()
    step = 384
    r.grad_in[...] = jnp.zeros((TOK, D), FULL)

    def feed(t, carry):
        wide = pl.ds(pl.multiple_of(t * step, 128), step)
        here = (lax.div(t * step, D), slice(None), pl.ds(pl.multiple_of(lax.rem(t * step, D), 128), step))
        up, down = r.v_up_weight[:, wide], r.v_down_weight[wide, :]
        act, slope = gelu_parts(dot(r.hidden2[...], up) + r.up_bias[:, wide])
        act = act.astype(HALF)
        r.act[here] = act
        r.final[...] += dot(act, down)
        d_pre = (dot_nt(r.cot[...], down) * slope).astype(HALF)
        r.d_pre[here] = d_pre
        r.up_sum[:, wide] = column_sum(d_pre.astype(FULL))
        r.grad_in[...] += dot_nt(d_pre, up)
        return carry

    lax.fori_loop(0, FF // step, feed, 0)
    r.encoded[0] = dot(gather, r.final[...].astype(HALF)).astype(HALF)

    def put(at, values, lo=0):
        r.vec[at : at + 1, lo : lo + values.shape[1]] = values

    r.vec[...] = jnp.zeros(r.vec.shape, FULL)
    cot = r.cot[...].astype(FULL)
    put(8, column_sum(cot))
    for k in range(FF // D):
        put(9 + k, r.up_sum[:, k * D : (k + 1) * D])

    grad = r.grad_in[...]
    put(6, column_sum(grad * r.nhat_two[...]))
    put(7, column_sum(grad))
    d_mid = cot + norm_back(grad, r.nhat_two[...], r.rstd_two[...], row(r.ln2_gain))
    r.stream[...] = d_mid
    r.d_attn[...] = d_mid.astype(HALF)
    put(5, column_sum(r.d_attn[...].astype(FULL)))
    r.d_mixed[...] = dot_nt(r.d_attn[...], r.v_out_weight[...]).astype(HALF)

    def attend_back(p, carry):
        query, key, value = (pair_of(r.qkv, k, p) for k in range(3))
        d_mixed = pair_of(r.d_mixed, 0, p)
        sides = [[], [], []]
        for h in range(2):
            probs = r.probs[2 * p + h]
            d_probs = dot_nt(only(d_mixed, h), value)
            delta = jnp.sum(d_probs * probs, -1, keepdims=True)
            d_scores = (probs * (d_probs - delta)).astype(HALF)
            sides[0].append(dot(d_scores, key) * 0.125)
            sides[1].append(dot_tn(d_scores, query))
            sides[2].append(dot_tn(probs.astype(HALF), d_mixed))
        for k in range(3):
            r.d_qkv[:, pl.ds(pl.multiple_of(k * D + p * 128, 128), 128)] = jnp.where(first, *sides[k]).astype(HALF)
        return carry

    lax.fori_loop(0, HEADS // 2, attend_back, 0)
    put(3, column_sum(r.d_qkv[:, :D].astype(FULL)))
    put(4, column_sum(r.d_qkv[:, 2 * D :].astype(FULL)))
    grad = dot_nt(r.d_qkv[...], r.v_qkv_weight[...])
    put(1, column_sum(grad * r.nhat_one[...]))
    put(2, column_sum(grad))
    d_stream = r.stream[...] + norm_back(grad, r.nhat_one[...], r.rstd_one[...], row(r.ln1_gain))
    r.text_grad[0] = d_stream[CELLS:]
    at_cell = iota((TOK, D), 0) < CELLS
    r.d_patches[...] = jnp.where(at_cell, d_stream, 0.0).astype(HALF).reshape(r.d_patches.shape)
    to_owners(r.d_patches, r.d_cells, 8)

    d_cells = r.d_cells[...].reshape(TOK, D)
    put(0, column_sum(d_cells.astype(FULL)))
    d_active = dot_nt(d_cells, r.v_embed_weight[...]).astype(HALF).astype(FULL)
    d_norm = d_active * r.slope[...]
    zhat = r.zhat[...]
    put(13, column_sum(d_norm * zhat))
    put(13, column_sum(d_norm), channels)
    d_hat = d_norm * row(r.gn_gain)
    back = exchange(image_sums(d_hat, d_hat * zhat), r.sums_back, 11) * entries
    d_feat = d_hat.reshape(images, cells, channels) - per_image(back, 0)
    d_feat = (d_feat - zhat.reshape(images, cells, channels) * per_image(back, 1)) * gscale
    d_feat = jnp.where(live, d_feat.reshape(TOK, channels), 0.0).astype(HALF)
    r.d_feat[...] = d_feat
    r.d_rows[:, 1 : rows + 1] = d_feat.reshape(images, rows, WIDE, channels)
    copies = edge_rows(r.d_rows, 14)
    d_feat = d_feat.astype(FULL)
    put(13, column_sum(r.tap_sum[:, :1] * d_feat) * (1.0 / taps), 2 * channels)
    put(14, column_sum(r.feat[...] * d_feat) * (1.0 / taps))
    for e, values in enumerate(shifted(edges_in(r.d_rows, copies))):
        r.d_views[e] = values.astype(HALF)
    grad = 0.0
    for a in range(3):
        for e in range(3):
            seen = window(r.d_views, 2 - a, 2 - e)
            grad = grad + dot_nt(seen, r.v_conv_weight[(3 * a + e) * channels : (3 * a + e + 1) * channels])
    grad = jnp.where(live, grad, 0.0).reshape(images, rows, WIDE, channels)
    r.image_grad[...] = grad[:, :, :GRID]

    swaps = {}
    base = 16

    def swap(name, at, src, dst):
        swaps.setdefault(name, []).append(send(src, dst, base + at, partner(CORE)))

    def swap_bands(name, at, src, dst):
        for y in range(2):
            swap(name, at + y, src.at[2 * y + 1 - core], dst.at[y])

    def banded(ref, src, width):
        for k in range(4):
            ref[k, :, :width] = src[:, k * width : (k + 1) * width]
            ref[k, :, width:] = jnp.zeros((TOK, ref.shape[2] - width), HALF)

    banded(r.mixed_bands, r.mixed, D // 4)
    banded(r.d_qkv_bands, r.d_qkv, 3 * D // 4)
    swap("down", 0, r.cot, r.r_cot)
    swap_bands("down", 1, r.act, r.r_act)
    swap("up", 3, r.hidden2, r.r_hidden2)
    swap_bands("up", 4, r.d_pre, r.r_d_pre)
    swap("qkv", 6, r.hidden, r.r_hidden)
    swap_bands("qkv", 7, r.d_qkv_bands, r.r_d_qkv)
    swap("out", 9, r.d_attn, r.r_d_attn)
    swap_bands("out", 10, r.mixed_bands, r.r_mixed)
    swap("conv", 12, r.views, r.r_views)
    swap("conv", 13, r.d_feat, r.r_d_feat)
    swap("emb", 14, r.active, r.r_active)
    swap("emb", 15, r.d_cells, r.r_d_cells)

    def arrived(name):
        for copy in swaps[name]:
            copy.wait_recv()

    pieces = {}
    slot = base + 16
    for (name, (plan, out, at)) in plans.items():
        refs = [getattr(r, f"{name}{k}") for k in range(1 + len(plan.order))]
        pieces[name] = Piece(plan, refs, (r.send_sem, r.recv_sem), slot, getattr(r, out), at)
        slot += len(plan.order)

    def unit(name, left, r_left, right, r_right, parts):
        arrived(name)
        for piece, lo in parts:
            piece = pieces[piece]
            w = piece.plan.width
            for y in range(2):
                for at in range(0, w, 128):
                    wide = slice(lo + at, lo + at + 128)
                    value = dot_tn(left[...], right[2 * y + core, :, wide])
                    value += dot_tn(r_left[...], r_right[y, :, wide])
                    value = value.astype(HALF).reshape(piece.plan.shape[1:-1] + (128,))
                    lead = (y,) + (slice(None),) * (len(piece.plan.shape) - 2)
                    piece.buf[lead + (slice(at, at + 128),)] = value
            piece.start()

    def columns(values, width):
        total = values.shape[1]
        col = iota((total, 2 * width), 1)
        want = jnp.where(col < width, col, col + width) + core * width
        pick = jnp.where(iota((total, 2 * width), 0) == want, 1.0, 0.0).astype(HALF)
        return dot(values, pick).astype(HALF)

    unit("down", r.cot, r.r_cot, r.act, r.r_act, [("p_da", 0), ("p_db", 384)])
    unit("up", r.hidden2, r.r_hidden2, r.d_pre, r.r_d_pre, [("p_ua", 0), ("p_ub", 384)])
    unit("qkv", r.hidden, r.r_hidden, r.d_qkv_bands, r.r_d_qkv, [("p_qa", 0), ("p_qb", 384)])
    unit("out", r.d_attn, r.r_d_attn, r.mixed_bands, r.r_mixed, [("p_o", 0)])
    arrived("conv")
    mine, theirs = columns(r.d_feat[...], channels // 4), columns(r.r_d_feat[...], channels // 4)
    piece = pieces["p_c"]
    for a in range(3):
        for e in range(3):
            value = dot_tn(window(r.views, a, e), mine) + dot_tn(window(r.r_views, a, e), theirs)
            value = value.astype(HALF)
            at, end = (3 * a + e) * channels, (3 * a + e + 1) * channels
            while at < end:
                block, lo = divmod(at, piece.plan.rows)
                size = min(end - at, piece.plan.rows - lo)
                where = tuple(block >> k & 1 for k in reversed(range(len(piece.plan.first))))
                done = at - (3 * a + e) * channels
                piece.buf[where + (slice(lo, lo + size),)] = value[done : done + size]
                at += size
    piece.start()
    arrived("emb")
    mine, theirs = columns(d_cells, D // 4), columns(r.r_d_cells[...].reshape(TOK, D), D // 4)
    piece = pieces["p_e"]
    value = dot_tn(r.active[...], mine) + dot_tn(r.r_active[...], theirs)
    piece.buf[...] = value.astype(HALF).reshape(piece.plan.shape)
    piece.start()

    def vec_start(stage):
        return send(r.vec if stage == 0 else r.vec_sum.at[stage - 1], r.vec_in.at[stage], slot + stage, partner(links[stage]))

    total = r.vec[...]
    on_way = vec_start(0)
    for stage in range(max([len(p.plan.order) for p in pieces.values()] + [len(links)])):
        for piece in pieces.values():
            if piece.stage < len(piece.plan.order):
                piece.step()
        if stage < len(links):
            on_way.wait_recv()
            total = total + r.vec_in[stage]
            if stage == len(links) - 1:
                r.o_vec[...] = total
            else:
                r.vec_sum[stage] = total
                on_way = vec_start(stage + 1)
    for piece in pieces.values():
        piece.drain()
    for copy in pending:
        copy.wait_send()


def body(
    image,
    conv_weight,
    gn_gain,
    gn_bias,
    embed_weight,
    embed_bias,
    ln1_gain,
    ln1_bias,
    qkv_weight,
    query_bias,
    value_bias,
    out_weight,
    out_bias,
    ln2_gain,
    ln2_bias,
    up_weight,
    up_bias,
    down_weight,
    down_bias,
    text_embed,
    text_len,
    cotangent,
):
    n_img, n_band = lax.axis_size("img"), lax.axis_size("band")
    img, band = lax.axis_index("img"), lax.axis_index("band")
    images, rows = image.shape[:2]
    taps, channels = conv_weight.shape
    img_bits = [("img", k) for k in bits(n_img)]
    y_first = [FAR] + img_bits
    x_first = img_bits[:1] + [FAR] + img_bits[1:]
    tail = img_bits + [FAR]
    plans = {
        "p_da": (Plan(n_img, D, 384, FAR, y_first), "o_down", 0),
        "p_db": (Plan(n_img, D, 384, FAR, x_first), "o_down", 384),
        "p_ua": (Plan(n_img, D, 384, FAR, y_first), "o_up", 0),
        "p_ub": (Plan(n_img, D, 384, FAR, x_first), "o_up", 384),
        "p_qa": (Plan(n_img, D, 384, FAR, y_first), "o_qkv", 0),
        "p_qb": (Plan(n_img, D, 256, FAR, x_first), "o_qkv", 384),
        "p_o": (Plan(n_img, D, 256, FAR, y_first), "o_out", 0),
        "p_c": (Plan(n_img, taps, channels // 2, None, tail), "o_conv", 0),
        "p_e": (Plan(n_img, channels, D // 2, None, tail), "o_emb", 0),
    }
    vec_shape = (16, D)
    arguments = {
        "image": image, "conv_weight": conv_weight, "gn_gain": gn_gain, "gn_bias": gn_bias, "embed_weight": embed_weight,
        "embed_bias": embed_bias, "ln1_gain": ln1_gain, "ln1_bias": ln1_bias, "qkv_weight": qkv_weight, "query_bias": query_bias,
        "value_bias": value_bias, "out_weight": out_weight, "out_bias": out_bias, "ln2_gain": ln2_gain, "ln2_bias": ln2_bias,
        "up_weight": up_weight, "up_bias": up_bias.reshape(1, FF), "down_weight": down_weight, "down_bias": down_bias,
        "text_embed": text_embed, "text_len": text_len, "cotangent": cotangent,
    }
    fetched = ("conv_weight", "embed_weight", "qkv_weight", "cotangent", "text_embed", "out_weight", "up_weight", "down_weight")
    spaces = {name: pl.ANY for name in fetched}
    spaces["text_len"] = pltpu.SMEM
    results = {
        "encoded": (cotangent.shape, HALF),
        "image_grad": (image.shape, FULL),
        "text_grad": (text_embed.shape, FULL),
        "o_down": ((plans["p_da"][0].rows, D), FULL),
        "o_up": ((plans["p_ua"][0].rows, D), FULL),
        "o_out": ((plans["p_o"][0].rows, 256), FULL),
        "o_qkv": ((plans["p_qa"][0].rows, 640), FULL),
        "o_conv": ((plans["p_c"][0].rows, channels // 2), FULL),
        "o_emb": ((plans["p_e"][0].rows, D // 2), FULL),
        "o_vec": (vec_shape, FULL),
        "o_wstat": ((2, channels), FULL),
    }
    halo = (images, rows + 2, WIDE, channels)
    split = (images, TOK // images, D)
    scratch = {
        "v_" + name: (arguments[name].shape, HALF) for name in fetched
    }
    scratch.update({
        "pixels": (halo, HALF), "views": ((3,) + halo, HALF), "feat": ((TOK, channels), FULL),
        "tap_sum": ((TOK, 128), FULL), "sums": ((n_band, 2 * images, channels), FULL), "sums_back": ((n_band, 2 * images, channels), FULL),
        "zhat": ((TOK, channels), FULL), "active": ((TOK, channels), HALF), "slope": ((TOK, channels), FULL),
        "embedded": (split, HALF), "patches": (split, HALF), "stream": ((TOK, D), FULL), "nhat_one": ((TOK, D), FULL),
        "rstd_one": ((TOK, 1), FULL), "hidden": ((TOK, D), HALF), "qkv": ((TOK, 3 * D), HALF), "probs": ((HEADS, TOK, TOK), FULL),
        "mixed": ((TOK, D), HALF), "nhat_two": ((TOK, D), FULL), "rstd_two": ((TOK, 1), FULL),
        "hidden2": ((TOK, D), HALF), "cot": ((TOK, D), HALF), "final": ((TOK, D), FULL), "grad_in": ((TOK, D), FULL),
        "act": ((4, TOK, D), HALF), "d_pre": ((4, TOK, D), HALF), "up_sum": ((1, FF), FULL), "vec": (vec_shape, FULL),
        "d_attn": ((TOK, D), HALF), "d_mixed": ((TOK, D), HALF), "d_qkv": ((TOK, 3 * D), HALF),
        "d_patches": (split, HALF), "d_cells": (split, HALF), "d_feat": ((TOK, channels), HALF), "d_rows": (halo, HALF),
        "d_views": ((3,) + halo, HALF), "mixed_bands": ((4, TOK, 256), HALF), "d_qkv_bands": ((4, TOK, 640), HALF),
        "r_cot": ((TOK, D), HALF), "r_act": ((2, TOK, D), HALF), "r_hidden2": ((TOK, D), HALF), "r_d_pre": ((2, TOK, D), HALF),
        "r_hidden": ((TOK, D), HALF), "r_d_qkv": ((2, TOK, 640), HALF), "r_d_attn": ((TOK, D), HALF), "r_mixed": ((2, TOK, 256), HALF),
        "r_views": ((3,) + halo, HALF), "r_d_feat": ((TOK, channels), HALF), "r_active": ((TOK, channels), HALF), "r_d_cells": (split, HALF),
    })
    slots = 32
    for name, (plan, _, _) in plans.items():
        for k, shape in enumerate(plan.scratch()):
            scratch[f"{name}{k}"] = (shape, HALF)
        slots += len(plan.order)
    n_links = 2 + len(img_bits)
    scratch["vec_sum"] = ((n_links,) + vec_shape, FULL)
    scratch["vec_in"] = ((n_links,) + vec_shape, FULL)
    slots += n_links
    sems = {"fetch_sem": 8, "send_sem": slots, "recv_sem": slots}
    names = list(arguments) + list(results) + list(scratch) + list(sems)
    whole = lambda space: pl.BlockSpec(memory_space=space)
    outs = pl.pallas_call(
        functools.partial(layer_kernel, names, plans),
        out_shape=[jax.ShapeDtypeStruct(*v) for v in results.values()],
        in_specs=[whole(spaces.get(name, pltpu.VMEM)) for name in arguments],
        out_specs=[whole(pltpu.VMEM)] * len(results),
        scratch_shapes=[pltpu.VMEM(*v) for v in scratch.values()] + [pltpu.SemaphoreType.DMA((n,)) for n in sems.values()],
        compiler_params=pltpu.CompilerParams(collective_id=0, has_side_effects=True, vmem_limit_bytes=63 * 2**20),
    )(*arguments.values())
    res = dict(zip(results, outs))
    vec = res["o_vec"]

    def own(v, total, axis=0):
        size = total // n_img
        return lax.dynamic_slice_in_dim(v, lax.rem(img, v.shape[axis] // size) * size, size, axis)

    def own_band(v, width):
        return lax.dynamic_slice_in_dim(v, lax.div(band, 2) * width, width, axis=1)

    def own_vec(at, lo=0, total=D):
        return own(vec[at, lo : lo + total], total)

    cols = channels // n_band
    taps_here = taps // n_img
    m_one, m_two = vec[13, 2 * channels :], vec[14, :channels]
    mine = lambda v: lax.dynamic_slice_in_dim(v, band * cols, cols)
    own_weight = lax.dynamic_slice(conv_weight, (img * taps_here, band * cols), (taps_here, cols)).astype(FULL)
    wmean, wscale = mine(res["o_wstat"][0]), mine(res["o_wstat"][1])
    own_stand = (own_weight - wmean) * wscale
    g_conv = own_band(own(res["o_conv"], taps), cols)
    g_conv = wscale * (g_conv - mine(m_one) - own_stand * mine(m_two))
    return (
        res["encoded"],
        res["image_grad"],
        res["text_grad"],
        g_conv,
        own_vec(13, 0, channels),
        own_vec(13, channels, channels),
        own_band(own(res["o_emb"], channels), D // n_band),
        own_vec(0),
        own_vec(1),
        own_vec(2),
        own(res["o_qkv"], D)[:, : 3 * D // n_band],
        own_vec(3),
        own_vec(4),
        own(res["o_out"], D)[:, : D // n_band].T,
        own_vec(5),
        own_vec(6),
        own_vec(7),
        own(res["o_up"], D),
        own(vec[9:13].reshape(FF), FF),
        own(res["o_down"], D).T,
        own_vec(8),
    )


def solution(mesh):
    in_specs = (
        P("img", "band", None, None),
        P(),
        P(),
        P(),
        P(),
        P(),
        P(),
        P(),
        P(),
        P(),
        P(),
        P(),
        P(),
        P(),
        P(),
        P(),
        P(),
        P(),
        P(),
        P(("img", "band"), None, None),
        P(("img", "band")),
        P(("img", "band"), None, None),
    )
    out_specs = (
        P(("img", "band"), None, None),
        P("img", "band", None, None),
        P(("img", "band"), None, None),
        P("img", "band"),
        P("img"),
        P("img"),
        P("img", "band"),
        P("img"),
        P("img"),
        P("img"),
        P("img", "band"),
        P("img"),
        P("img"),
        P("band", "img"),
        P("img"),
        P("img"),
        P("img"),
        P("img", "band"),
        P("img"),
        P("band", "img"),
        P("img"),
    )
    return jax.shard_map(body, mesh=mesh, in_specs=in_specs, out_specs=out_specs, check_vma=False)
```

time: 970 us -> 186 us (0.19)
  waiting for transfers between devices: 724 us -> 0 us
  Pallas kernels: 0 us -> 160 us
  blocking collectives: 68.4 us -> 0 us
  matrix products: 57 us -> 0 us
  local copies, waits for them, and re-layouts: 60.4 us -> 22.4 us
  other arithmetic: 23 us -> 1.08 us
  between operations: 18.9 us -> 1.36 us
  starting transfers between devices: 12 us -> 0 us
    reduce_scatter x8 -> x0, waiting for transfers between devices: 633 us -> none  [the longest x1 166 us: body(): lax.psum_scatter(g_down_w, 'img', scatter_dimension=1, tiled=True)]
    pallas_call x0 -> x1, Pallas kernels: none -> 160 us  [body(): pl.pallas_call(functools.partial(layer_kernel, names, plans), out_shape=[...]
    unnamed x16 -> x0, waiting for transfers between devices: 84.4 us -> none
    dot_general x30 -> x0, matrix products: 54 us -> none  [the longest x24 47.1 us: matmul(): return jnp.dot(left, right, preferred_element_type=jnp.float32)]
    unnamed x1 -> x0, blocking collectives: 38 us -> none
    psum x2 -> x0, blocking collectives: 20.6 us -> none  [the longest x1 11.1 us: body(): back_one, back_two = lax.psum((back_one, back_two), 'band')]
    reduce_sum x18 -> x0, other arithmetic: 10.7 us -> none  [the longest x1 1.64 us: body(): wscale = lax.rsqrt(jnp.mean(wcent * wcent, 0) + 1e-05)]
    unnamed x231 -> x11, local copies, waits for them, and re-layouts: 22.6 us -> 12.2 us
  transfers between devices with their start and end apart: 17 -> 0, of which waited for: 12 -> 0; matrix products, arithmetic and copies ran while one was open for 5% -> 0% of each run, Pallas kernels for 0% -> 0%
where the time goes in v2:
time: 186 us; the launch traced here: 185 us
  Pallas kernels  160 us (86%)
  local copies, waits for them, and re-layouts  22.4 us (12%)
    pallas_call x1, Pallas kernels, body(): pl.pallas_call(functools.partial(layer_kernel, names, plans), out_shape=[...  160 us
    unnamed x11, local copies, waits for them, and re-layouts  12.2 us
    dynamic_slice x8, local copies, waits for them, and re-layouts, own(): lax.dynamic_slice_in_dim(v, lax.rem(img, v.shape[axis] // size) * size, s...  4.75 us

profile of v2, /device:TPU:0, one launch (start us, length us, event | category | flops | bytes accessed | tf_op | source)
XLA Modules:
  0.0 185.3 jit_solution(16480401390186344921)
XLA Ops:
  0.7 1.6 copy.43.refs_0_
  2.9 160.5 %shard_map.373 = (bf16[1,228,768]{2,1,0:T(8,128)(2,1)}, f32[4,4,14,256]{3,2,1,0:T(8,128)}, f32[1,32,768]{2,1,0:T(8,128)}, f32[96,768]{1,0:T(8,128)}, f32[96,768]...) custom-call(bf16[4,4,14,256]{3,2,1,0:T(8,128)(2,1)} %copy.43.refs_0_, ...), custom_call_target="tpu_custom_call" | custom-call | tf_op jit(solution)/shard_map/pallas_call | solution.py:671
  163.4 0.0 copy-start
  163.4 1.2 fusion.15
  164.6 0.6 fusion.12
  165.2 0.6 fusion.10
  165.8 0.6 fusion.8
  166.4 0.6 fusion.6
  167.0 0.8 fusion.16
  167.8 0.1 fusion
  167.8 0.1 fusion.1
  167.9 0.1 fusion.2
  168.0 0.1 fusion.3
  168.0 1.1 subtract_multiply_fusion
  169.1 0.8 copy.45
  169.9 0.6 fusion.4
  170.5 0.6 fusion.5
  171.1 0.6 fusion.14
  171.6 0.7 slice.70
  172.4 0.7 dynamic_slice.112
  173.0 1.5 constant_dynamic-slice_fusion.9
  174.5 1.8 copy.44
  176.3 0.9 slice_bitcast_fusion
  177.2 0.7 copy.46
  178.0 1.7 copy.53
  179.7 1.5 copy.54
  181.2 1.7 copy.55
  182.9 1.7 copy.56
  184.6 0.0 copy-done
  184.6 0.7 copy.57
  (1 shorter events, 0.0 us)
Async XLA Ops:
  163.4 21.2 %copy-start = (f32[96,768]{1,0:T(8,128)S(1)}, f32[96,768]{1,0:T(8,128)}, u32[]{:S(2)}) copy-start(f32[96,768]{1,0:T(8,128)} %get-tuple-element.42) | copy-start | bytes 884740

commit v3 on v2

v3 whole, which is shorter than its diff:
```python
import functools
import types

import jax
import jax.numpy as jnp
from jax import lax
from jax.experimental import pallas as pl
from jax.experimental.pallas import tpu as pltpu
from jax.sharding import PartitionSpec as P

D = 768
FF = 3072
HEADS = 12
GROUPS = 32
GRID = 14
TEXT = 32
PATCHES = 196
WIDE = 16
TOK = 256
CELLS = GRID * WIDE
HALF = jnp.bfloat16
FULL = jnp.float32
MESH_ID = pl.DeviceIdType.MESH
CORE = ("band", 1)
FAR = ("band", 2)


def bit_of(value, bit):
    return lax.rem(lax.div(value, bit), 2)


def flip(value, bit):
    return value + bit * (1 - 2 * bit_of(value, bit))


def partner(label):
    axis, bit = label
    img, band = lax.axis_index("img"), lax.axis_index("band")
    return (flip(img, bit), band) if axis == "img" else (img, flip(band, bit))


def my_bit(label):
    axis, bit = label
    return bit_of(lax.axis_index(axis), bit)


def bits(count):
    return [1 << k for k in range(count.bit_length() - 1)]


class Plan:
    def __init__(self, n_img, rows, width, lead, order, parts=1):
        self.width = width
        split = [("img", k) for k in reversed(bits(n_img)) if (rows // n_img) * k % 16 == 0]
        self.rows = (rows >> len(split)) // parts
        self.first = ([lead] if lead else []) + split
        rest = [("img", k) for k in bits(n_img) if ("img", k) not in split]
        ordered = [lab for lab in order if lab in self.first]
        self.order = ordered + rest + [lab for lab in order if lab not in self.first and lab[0] == "band"]
        self.shapes = []
        labels = list(self.first)
        for lab in self.order:
            if lab in labels:
                labels.remove(lab)
            self.shapes.append((2,) * len(labels) + (self.rows, width))
        self.shape = (2,) * len(self.first) + (self.rows, width)

    def scratch(self):
        return [self.shape] + self.shapes


class Once:
    def __init__(self, copy):
        self.copy, self.left = copy, {"wait", "wait_send", "wait_recv"}
        copy.start()

    def _wait(self, kind):
        if kind in self.left:
            self.left.remove(kind)
            getattr(self.copy, kind)()

    def wait(self):
        self._wait("wait")

    def wait_send(self):
        self._wait("wait_send")

    def wait_recv(self):
        self._wait("wait_recv")


class Piece:
    def __init__(self, plan, refs, sems, slot, out, at, pending):
        self.pending = pending
        self.plan, self.buf, self.recv = plan, refs[0], refs[1:]
        self.sems, self.slot = sems, slot
        self.labels, self.cur = list(plan.first), refs[0]
        self.sent = []
        self.out = out.at[pl.ds(at[0], plan.rows), pl.ds(at[1], plan.width)]
        self.stage = 0

    def _index(self, label, which):
        at = self.labels.index(label)
        return (slice(None),) * at + (which,)

    def start(self):
        label = self.plan.order[self.stage]
        src = self.cur
        if label in self.labels:
            src = src.at[self._index(label, 1 - my_bit(label))]
        send, recv = self.sems
        copy = pltpu.make_async_remote_copy(
            src_ref=src,
            dst_ref=self.recv[self.stage],
            send_sem=send.at[self.slot + self.stage],
            recv_sem=recv.at[self.slot + self.stage],
            device_id=partner(label),
            device_id_type=MESH_ID,
        )
        self.sent.append(Once(copy))
        self.pending.append(self.sent[-1])

    def step(self):
        label = self.plan.order[self.stage]
        self.sent[self.stage].wait_recv()
        mine = self.cur
        if label in self.labels:
            mine = mine[self._index(label, my_bit(label))]
            self.labels.remove(label)
        else:
            mine = mine[...]
        got = self.recv[self.stage]
        self.stage += 1
        if self.stage == len(self.plan.order):
            self.out[...] = (got[...].astype(FULL) + mine.astype(FULL)).reshape(self.out.shape)
        else:
            got[...] = got[...] + mine
            self.cur = got
            self.start()


def dot(left, right):
    return jnp.dot(left, right, preferred_element_type=FULL)


def dot_tn(left, right):
    return lax.dot_general(left, right, (((0,), (0,)), ((), ())), preferred_element_type=FULL)


def dot_nt(left, right):
    return lax.dot_general(left, right, (((1,), (1,)), ((), ())), preferred_element_type=FULL)


def exact_dot(left, right):
    return jnp.dot(left, right, precision=lax.Precision.HIGHEST, preferred_element_type=FULL)


def gelu_parts(x):
    cdf = 0.5 + 0.5 * lax.erf(x * 0.7071067811865476)
    pdf = jnp.exp(-0.5 * x * x) * 0.3989422804014327
    return x * cdf, cdf + x * pdf


def iota(shape, axis):
    return lax.broadcasted_iota(jnp.int32, shape, axis)


def row(ref):
    return ref[...].reshape(1, -1)


def column_sum(values):
    return jnp.sum(values, 0, keepdims=True)


def shifted(values):
    edge = jnp.zeros(values.shape[:2] + (1, values.shape[3]), FULL)
    left = jnp.concatenate([edge, values[:, :, : WIDE - 1]], 2)
    right = jnp.concatenate([values[:, :, 1:], edge], 2)
    return left, values, right


DOWN, UP, QKV, TAIL = ("p_d0", "p_d1", "p_d2"), ("p_u0", "p_u1", "p_u2"), ("p_q0", "p_q1", "p_q2"), ("p_c0", "p_c1", "p_c2", "p_e")
POLLS = {
    "back1": DOWN,
    "cells": ("qkv",) + UP + ("+p_q1", "+p_q2"),
    "sums": ("p_d1",),
    "edges": ("p_d0", "p_d2", "p_u1", "+p_q0"),
    "grad": ("p_u0", "p_u2"),
    "end": DOWN + ("p_q1", "p_q2", "p_q0") + TAIL + UP + DOWN + ("vec",) + QKV + TAIL + UP + ("vec",) + QKV + ("vec",) + TAIL + QKV + ("vec",) + TAIL + ("vec",),
}


def layer_kernel(names, plans, *refs):
    r = types.SimpleNamespace(**dict(zip(names, refs)))
    img, band = lax.axis_index("img"), lax.axis_index("band")
    n_img, n_band = lax.axis_size("img"), lax.axis_size("band")
    images, rows = r.image.shape[:2]
    channels = r.conv_weight.shape[1]
    core = my_bit(CORE)
    others = [lax.rem(band + d, n_band) for d in range(n_band)]

    fetches = {}

    def fetch(name, at):
        copy = pltpu.make_async_copy(getattr(r, name), getattr(r, "v_" + name), r.fetch_sem.at[at])
        fetches[name] = Once(copy)

    for at, name in enumerate(("conv_weight", "embed_weight", "qkv_weight", "cotangent", "text_embed", "out_weight", "up_weight", "down_weight")):
        fetch(name, at)

    links = [CORE, FAR] + [("img", k) for k in bits(n_img)]
    barrier = pltpu.get_barrier_semaphore()
    for d in range(1, n_band):
        pl.semaphore_signal(barrier, inc=1, device_id=(img, others[d]), device_id_type=MESH_ID)
    for label in links[2:]:
        pl.semaphore_signal(barrier, inc=1, device_id=partner(label), device_id_type=MESH_ID)
    pl.semaphore_wait(barrier, n_band - 1 + len(links) - 2)

    pending = []

    def send(src, dst, at, device):
        copy = pltpu.make_async_remote_copy(
            src_ref=src, dst_ref=dst, send_sem=r.send_sem.at[at], recv_sem=r.recv_sem.at[at],
            device_id=device, device_id_type=MESH_ID)
        pending.append(Once(copy))
        return pending[-1]

    def edge_rows(ref, at):
        up = send(ref.at[:, rows], ref.at[:, 0], at, (img, others[1]))
        down = send(ref.at[:, 1], ref.at[:, rows + 1], at + 1, (img, others[n_band - 1]))
        return up, down

    def edges_in(ref, copies):
        for copy in copies:
            copy.wait_recv()
        values = ref[...].astype(FULL)
        at = iota(values.shape, 1) + band * rows
        return jnp.where((at == 0) | (at > n_band * rows), 0.0, values)

    def exchange(values, slots, at, meanwhile=None):
        slots[0] = values
        copies = [send(slots.at[0], slots.at[d], at + d - 1, (img, others[d])) for d in range(1, n_band)]
        poll(meanwhile)
        for d, copy in enumerate(copies, 1):
            copy.wait_recv()
            values = values + slots[d]
        return values

    def to_owners(src, dst, at, meanwhile=None):
        copies = [send(src.at[others[d]], dst.at[band], at + d - 1, (img, others[d])) for d in range(1, n_band)]
        dst[band] = src[band]
        poll(meanwhile)
        for copy in copies:
            copy.wait_recv()

    swaps = {}
    base = 16

    def swap(name, at, src, dst):
        swaps.setdefault(name, []).append(send(src, dst, base + at, partner(CORE)))

    def swap_bands(name, at, src, dst):
        for y in range(2):
            swap(name, at + y, src.at[2 * y + 1 - core], dst.at[y])

    def swap_left(name, at, ref):
        swap(name, at, ref.at[:, pl.ds(0, TOK)], ref.at[:, pl.ds(TOK, TOK)])

    def arrived(name):
        for copy in swaps[name]:
            copy.wait_recv()

    pieces = {}
    slot = base + 16
    for name, (plan, out, at) in plans.items():
        refs = [getattr(r, f"{name}_{k}") for k in range(1 + len(plan.order))]
        pieces[name] = Piece(plan, refs, (r.send_sem, r.recv_sem), slot, getattr(r, out), at, pending)
        slot += len(plan.order)

    down, up, qkv = DOWN, UP, QKV

    def poll(point):
        for name in POLLS.get(point, ()):
            if name[0] == "+":
                pieces[name[1:]].start()
            elif name == "vec":
                vec_step()
            elif name == "qkv":
                qkv_unit()
            else:
                advance(name)

    def advance(*names):
        for name in names:
            if pieces[name].stage < len(pieces[name].plan.order):
                pieces[name].step()

    def unit(parts, terms, start=True):
        for j, name in enumerate(parts):
            piece = pieces[name]
            wide = slice(256 * j, 256 * (j + 1))
            for y in range(2):
                value = 0.0
                for left, right, got, at in terms:
                    if j >= at:
                        cut = slice(256 * (j - at), 256 * (j - at + 1))
                        both = jnp.concatenate([right[2 * y + core, :, cut], got[y, :, cut]], 0)
                        value = value + dot(left[...], both)
                piece.buf[y] = value.astype(HALF).reshape(piece.plan.shape[1:])
            if start:
                piece.start()

    r.pixels[:, 1 : rows + 1, GRID:, :] = jnp.zeros((images, rows, WIDE - GRID, channels), HALF)
    at_row = iota((images, rows, GRID, channels), 1) + band * rows
    r.pixels[:, 1 : rows + 1, :GRID, :] = jnp.where(at_row < GRID, r.image[...].astype(FULL), 0.0).astype(HALF)
    copies = edge_rows(r.pixels, 0)

    fetches["cotangent"].wait()
    seq = r.cotangent.shape[1]

    def token_of(at):
        return jnp.where(at < CELLS, jnp.where(lax.rem(at, WIDE) < GRID, lax.div(at, WIDE) * GRID + lax.rem(at, WIDE), -1), at - CELLS + PATCHES)

    spread = jnp.where(token_of(iota((TOK, seq), 0)) == iota((TOK, seq), 1), 1.0, 0.0).astype(HALF)
    gather = jnp.where(token_of(iota((seq, TOK), 1)) == iota((seq, TOK), 0), 1.0, 0.0).astype(HALF)
    r.cot[...] = dot(spread, r.v_cotangent[0]).astype(HALF)

    r.t_cot[:, :TOK] = r.cot[...].T
    swap_left("down", 0, r.t_cot)

    fetches["conv_weight"].wait()
    taps = r.conv_weight.shape[0]
    chunks = [slice(k, k + 256) for k in range(0, taps, 256)]
    wmean = sum(column_sum(r.v_conv_weight[s].astype(FULL)) for s in chunks) * (1.0 / taps)
    wvar = 0.0
    for s in chunks:
        cent = r.v_conv_weight[s].astype(FULL) - wmean
        wvar = wvar + column_sum(cent * cent)
    wscale = lax.rsqrt(wvar * (1.0 / taps) + 1e-05)
    taps_here = taps // n_img
    if taps_here % 16 == 0:
        own = r.v_conv_weight[pl.ds(pl.multiple_of(img * taps_here, 16), taps_here)]
    else:
        own = jnp.where(iota((taps_here, taps), 1) == iota((taps_here, taps), 0) + img * taps_here, 1.0, 0.0).astype(HALF)
        own = dot(own, r.v_conv_weight[...]).astype(HALF)
    own = ((own.astype(FULL) - wmean) * wscale, jnp.broadcast_to(wscale, (8, channels)))
    r.o_wstat[...] = jnp.concatenate(own, 0)
    for s in chunks:
        r.v_conv_weight[s] = ((r.v_conv_weight[s].astype(FULL) - wmean) * wscale).astype(HALF)
    pixels = edges_in(r.pixels, copies)
    for e, values in enumerate(shifted(pixels)):
        r.views[e] = values.astype(HALF)

    def window(views, a, e):
        return views[e, :, a : a + rows].reshape(TOK, channels)

    place = iota((TOK, channels), 0)
    live = (lax.rem(place, WIDE) < GRID) & (lax.rem(lax.div(place, WIDE), rows) + band * rows < GRID)
    feat = 0.0
    tap_sum = 0.0
    for a in range(3):
        for e in range(3):
            seen = window(r.views, a, e)
            feat = feat + dot(seen, r.v_conv_weight[(3 * a + e) * channels : (3 * a + e + 1) * channels])
            tap_sum = tap_sum + seen.astype(FULL)
    feat = jnp.where(live, feat, 0.0)
    r.feat[...] = feat
    r.tap_sum[...] = jnp.broadcast_to(jnp.sum(tap_sum, 1, keepdims=True), (TOK, 128))
    per_group = channels // GROUPS
    entries = 1.0 / (GRID * GRID * per_group)
    same = lax.div(iota((channels, channels), 0), per_group) == lax.div(iota((channels, channels), 1), per_group)
    same = jnp.where(same, 1.0, 0.0)
    cells = TOK // images

    def image_sums(one, two):
        one = jnp.sum(one.reshape(images, cells, channels), 1)
        two = jnp.sum(two.reshape(images, cells, channels), 1)
        return exact_dot(jnp.concatenate([one, two], 0), same)

    def per_image(sums, which):
        return sums[which * images : (which + 1) * images].reshape(images, 1, channels)
    sums = exchange(image_sums(feat, feat * feat), r.sums, 2) * entries
    gmean = per_image(sums, 0)
    gscale = lax.rsqrt(per_image(sums, 1) - gmean * gmean + 1e-05)
    zhat = ((feat.reshape(images, cells, channels) - gmean) * gscale).reshape(TOK, channels)
    r.zhat[...] = zhat
    stem, slope = gelu_parts(zhat * row(r.gn_gain) + row(r.gn_bias))
    r.active[...] = jnp.where(live, stem, 0.0).astype(HALF)
    r.slope[...] = jnp.where(live, slope, 0.0)
    fetches["embed_weight"].wait()
    embedded = dot(r.active[...], r.v_embed_weight[...]) + row(r.embed_bias)
    r.embedded[...] = embedded.astype(HALF).reshape(images, cells, D)
    to_owners(r.embedded, r.patches, 5)
    def norm(values):
        mean = jnp.mean(values, -1, keepdims=True)
        cent = values - mean
        rstd = lax.rsqrt(jnp.mean(cent * cent, -1, keepdims=True) + 1e-06)
        return cent * rstd, rstd

    def norm_back(grad, nhat, rstd, gain):
        s = grad * gain
        inner = s - jnp.mean(s, -1, keepdims=True) - nhat * jnp.mean(s * nhat, -1, keepdims=True)
        return inner * rstd

    fetches["text_embed"].wait()
    r.stream[...] = r.patches[...].reshape(TOK, D).astype(FULL)
    r.stream[CELLS:] = r.v_text_embed[0].astype(FULL)
    nhat, rstd_one = norm(r.stream[...])
    r.nhat_one[...] = nhat
    r.rstd_one[...] = rstd_one
    r.hidden[...] = (nhat * row(r.ln1_gain) + row(r.ln1_bias)).astype(HALF)
    r.t_hidden[:, :TOK] = r.hidden[...].T
    swap_left("qkv", 6, r.t_hidden)
    fetches["qkv_weight"].wait()
    for k, bias in enumerate((r.query_bias, None, r.value_bias)):
        values = dot(r.hidden[...], r.v_qkv_weight[:, k * D : (k + 1) * D])
        if bias is not None:
            values = values + row(bias)
        values = values.astype(HALF)
        r.qkv[:, k * D : (k + 1) * D] = values * 0.125 if k == 0 else values
    key_at = iota((1, TOK), 1)
    key_live = ((key_at < CELLS) & (lax.rem(key_at, WIDE) < GRID)) | ((key_at >= CELLS) & (key_at - CELLS < r.text_len[0]))
    first = iota((TOK, 128), 1) < 64
    zero = jnp.zeros((TOK, 128), HALF)

    def pair_of(ref, k, p):
        return ref[:, pl.ds(pl.multiple_of(k * D + p * 128, 128), 128)]

    def only(values, h):
        return jnp.where(first, values, zero) if h == 0 else jnp.where(first, zero, values)

    def attend(p, carry):
        query, key, value = (pair_of(r.qkv, k, p) for k in range(3))
        sides = []
        for h in range(2):
            scores = jnp.where(key_live, dot_nt(only(query, h), key), -1000000000.0)
            expd = jnp.exp(scores - jnp.max(scores, -1, keepdims=True))
            probs = expd * (1.0 / jnp.sum(expd, -1, keepdims=True))
            probs = probs.astype(HALF)
            r.probs[2 * p + h] = probs
            sides.append(dot(probs, value))
        r.mixed[:, pl.ds(pl.multiple_of(p * 128, 128), 128)] = jnp.where(first, *sides).astype(HALF)
        return carry

    lax.fori_loop(0, HEADS // 2, attend, 0)
    for k in range(4):
        width = D // 4
        r.mixed_bands[k] = jnp.concatenate([jnp.zeros((TOK, 256 - width), HALF), r.mixed[:, k * width : (k + 1) * width]], 1)
    swap_bands("out", 10, r.mixed_bands, r.r_mixed)
    fetches["out_weight"].wait()
    mid = r.stream[...] + dot(r.mixed[...], r.v_out_weight[...]) + row(r.out_bias)
    r.final[...] = mid + row(r.down_bias)
    nhat, rstd_two = norm(mid)
    r.nhat_two[...] = nhat
    r.rstd_two[...] = rstd_two
    r.hidden2[...] = (nhat * row(r.ln2_gain) + row(r.ln2_bias)).astype(HALF)
    fetches["up_weight"].wait()
    r.t_hidden2[:, :TOK] = r.hidden2[...].T
    swap_left("up", 3, r.t_hidden2)

    def feed(k, carry):
        wide = pl.ds(pl.multiple_of(k * D, 128), D)
        act, slope = gelu_parts(dot(r.hidden2[...], r.v_up_weight[:, wide]) + r.up_bias[:, wide])
        r.act[k] = act.astype(HALF)
        r.slopes[k] = slope.astype(HALF)
        return carry

    lax.fori_loop(0, FF // D, feed, 0)
    swap_bands("down", 1, r.act, r.r_act)
    fetches["down_weight"].wait()
    final = r.final[...]
    for k in range(FF // D):
        final = final + dot(r.act[k], r.v_down_weight[k * D : (k + 1) * D])
    r.encoded[0] = dot(gather, final.astype(HALF)).astype(HALF)
    arrived("down")
    unit(down, [(r.t_cot, r.act, r.r_act, 0)])

    def feed_back(k, carry):
        wide = pl.ds(pl.multiple_of(k * D, 128), D)
        d_pre = dot_nt(r.cot[...], r.v_down_weight[wide, :]) * r.slopes[k].astype(FULL)
        r.d_pre[k] = d_pre.astype(HALF)
        r.up_sum[k] = column_sum(r.d_pre[k].astype(FULL))
        return carry

    lax.fori_loop(0, FF // D, feed_back, 0)
    swap_bands("up", 4, r.d_pre, r.r_d_pre)
    grad = 0.0
    for k in range(FF // D):
        grad = grad + dot_nt(r.d_pre[k], r.v_up_weight[:, k * D : (k + 1) * D])
    r.final[...] = grad
    def put(at, values, lo=0):
        r.vec[at : at + 1, lo : lo + values.shape[1]] = values

    r.vec[...] = jnp.zeros(r.vec.shape, FULL)
    cot = r.cot[...].astype(FULL)
    put(8, column_sum(cot))
    for k in range(FF // D):
        put(9 + k, r.up_sum[k])

    grad = r.final[...]
    put(6, column_sum(grad * r.nhat_two[...]))
    put(7, column_sum(grad))
    d_mid = cot + norm_back(grad, r.nhat_two[...], r.rstd_two[...], row(r.ln2_gain))
    r.stream[...] = d_mid
    r.d_attn[...] = d_mid.astype(HALF)
    r.t_attn[:, :TOK] = r.d_attn[...].T
    swap_left("out", 9, r.t_attn)
    put(5, column_sum(r.d_attn[...].astype(FULL)))
    r.d_mixed[...] = dot_nt(r.d_attn[...], r.v_out_weight[...]).astype(HALF)

    arrived("up")
    unit(up, [(r.t_hidden2, r.d_pre, r.r_d_pre, 0)])
    def attend_back(p, carry):
        query, key, value = (pair_of(r.qkv, k, p) for k in range(3))
        d_mixed = pair_of(r.d_mixed, 0, p)
        sides = [[], [], []]
        for h in range(2):
            probs = r.probs[2 * p + h]
            d_probs = dot_nt(only(d_mixed, h), value)
            weight = probs.astype(FULL)
            delta = jnp.sum(d_probs * weight, -1, keepdims=True)
            d_scores = (weight * (d_probs - delta)).astype(HALF)
            sides[0].append(dot(d_scores, key) * 0.125)
            sides[1].append(dot_tn(d_scores, query))
            sides[2].append(dot_tn(probs, d_mixed))
        for k in range(3):
            r.d_qkv[:, pl.ds(pl.multiple_of(k * D + p * 128, 128), 128)] = jnp.where(first, *sides[k]).astype(HALF)
        return carry

    for part in range(3):
        lax.fori_loop(HEADS // 6 * part, HEADS // 6 * (part + 1), attend_back, 0)
        poll(f"back{part}")
    for k in range(4):
        width = 3 * D // 4
        r.d_qkv_bands[k] = jnp.concatenate([r.d_qkv[:, k * width : (k + 1) * width], jnp.zeros((TOK, D - width), HALF)], 1)
    swap_bands("qkv", 7, r.d_qkv_bands, r.r_d_qkv)
    put(3, column_sum(r.d_qkv[:, :D].astype(FULL)))
    put(4, column_sum(r.d_qkv[:, 2 * D :].astype(FULL)))
    grad = dot_nt(r.d_qkv[...], r.v_qkv_weight[...])
    put(1, column_sum(grad * r.nhat_one[...]))
    put(2, column_sum(grad))
    d_stream = r.stream[...] + norm_back(grad, r.nhat_one[...], r.rstd_one[...], row(r.ln1_gain))
    r.text_grad[0] = d_stream[CELLS:]
    at_cell = iota((TOK, D), 0) < CELLS
    r.d_patches[...] = jnp.where(at_cell, d_stream, 0.0).astype(HALF).reshape(r.d_patches.shape)
    def qkv_unit():
        arrived("qkv")
        arrived("out")
        unit(qkv, [(r.t_hidden, r.d_qkv_bands, r.r_d_qkv, 0), (r.t_attn, r.mixed_bands, r.r_mixed, 2)], False)
    to_owners(r.d_patches, r.d_cells, 8, "cells")
    d_cells = r.d_cells[...].reshape(TOK, D)
    put(0, column_sum(d_cells.astype(FULL)))
    d_active = dot_nt(d_cells, r.v_embed_weight[...]).astype(HALF).astype(FULL)
    d_norm = d_active * r.slope[...]
    zhat = r.zhat[...]
    put(13, column_sum(d_norm * zhat))
    put(13, column_sum(d_norm), channels)
    d_hat = d_norm * row(r.gn_gain)
    back = exchange(image_sums(d_hat, d_hat * zhat), r.sums_back, 11, "sums") * entries
    d_feat = d_hat.reshape(images, cells, channels) - per_image(back, 0)
    d_feat = (d_feat - zhat.reshape(images, cells, channels) * per_image(back, 1)) * gscale
    d_feat = jnp.where(live, d_feat.reshape(TOK, channels), 0.0).astype(HALF)
    r.d_feat[...] = d_feat
    r.d_rows[:, 1 : rows + 1] = d_feat.reshape(images, rows, WIDE, channels)
    copies = edge_rows(r.d_rows, 14)
    d_feat = d_feat.astype(FULL)
    put(13, column_sum(r.tap_sum[:, :1] * d_feat) * (1.0 / taps), 2 * channels)
    put(14, column_sum(r.feat[...] * d_feat) * (1.0 / taps))

    def vec_start(stage):
        return send(r.vec if stage == 0 else r.vec_sum.at[stage - 1], r.vec_in.at[stage], slot + stage, partner(links[stage]))

    vec_state = [r.vec[...], 0, vec_start(0)]

    def vec_step():
        total, stage, on_way = vec_state
        on_way.wait_recv()
        total = total + r.vec_in[stage]
        if stage == len(links) - 1:
            r.o_vec[...] = total
        else:
            r.vec_sum[stage] = total
            on_way = vec_start(stage + 1)
        vec_state[:] = [total, stage + 1, on_way]

    poll("edges")
    for e, values in enumerate(shifted(edges_in(r.d_rows, copies))):
        r.d_views[e] = values.astype(HALF)
    grad = 0.0
    for a in range(3):
        for e in range(3):
            seen = window(r.d_views, 2 - a, 2 - e)
            grad = grad + dot_nt(seen, r.v_conv_weight[(3 * a + e) * channels : (3 * a + e + 1) * channels])
    grad = jnp.where(live, grad, 0.0).reshape(images, rows, WIDE, channels)
    r.image_grad[...] = grad[:, :, :GRID]

    poll("grad")
    swap("conv", 12, r.views, r.r_views)
    swap("conv", 13, r.d_feat, r.r_d_feat)
    swap("emb", 14, r.active, r.r_active)
    swap("emb", 15, r.d_cells, r.r_d_cells)

    def columns(values, width):
        total = values.shape[1]
        col = iota((total, 2 * width), 1)
        want = jnp.where(col < width, col, col + width) + core * width
        pick = jnp.where(iota((total, 2 * width), 0) == want, 1.0, 0.0).astype(HALF)
        return dot(values, pick).astype(HALF)

    arrived("conv")
    mine, theirs = columns(r.d_feat[...], channels // 4), columns(r.r_d_feat[...], channels // 4)
    rows_here = pieces["p_c0"].plan.rows
    for a in range(3):
        for e in range(3):
            value = dot_tn(window(r.views, a, e), mine) + dot_tn(window(r.r_views, a, e), theirs)
            value = value.astype(HALF)
            begin = at = (3 * a + e) * channels
            while at < begin + channels:
                line, lo = divmod(at, rows_here)
                block, part = divmod(line, 3)
                size = min(begin + channels - at, rows_here - lo)
                piece = pieces[f"p_c{part}"]
                where = tuple(block >> k & 1 for k in reversed(range(len(piece.plan.first))))
                piece.buf[where + (slice(lo, lo + size),)] = value[at - begin : at - begin + size]
                at += size
    for part in range(3):
        pieces[f"p_c{part}"].start()
    arrived("emb")
    mine, theirs = columns(d_cells, D // 4), columns(r.r_d_cells[...].reshape(TOK, D), D // 4)
    piece = pieces["p_e"]
    value = dot_tn(r.active[...], mine) + dot_tn(r.r_active[...], theirs)
    piece.buf[...] = value.astype(HALF).reshape(piece.plan.shape)
    piece.start()
    poll("end")
    while vec_state[1] < len(links) or any(p.stage < len(p.plan.order) for p in pieces.values()):
        advance(*pieces)
        if vec_state[1] < len(links):
            vec_step()
    for copy in pending:
        copy.wait_send()


def finish_kernel(names, *refs):
    r = types.SimpleNamespace(**dict(zip(names, refs)))
    img, band = lax.axis_index("img"), lax.axis_index("band")
    n_img, n_band = lax.axis_size("img"), lax.axis_size("band")
    far = my_bit(FAR)
    for name in ("encoded", "image_grad", "text_grad"):
        getattr(r, name)[...] = getattr(r, "i_" + name)[...]

    def own(ref, rows):
        if ref.shape[0] == rows:
            return ref[...]
        at = lax.rem(img, ref.shape[0] // rows) * rows
        pick = jnp.where(iota((rows, ref.shape[0]), 1) == iota((rows, ref.shape[0]), 0) + at, 1.0, 0.0)
        return exact_dot(pick, ref[...])

    def lanes(values, at, count):
        width = values.shape[1]
        return exact_dot(values, jnp.where(iota((width, count), 0) == iota((width, count), 1) + at, 1.0, 0.0))

    def half(values):
        width = values.shape[1] // 2
        return jnp.where(far == 0, values[:, :width], values[:, width:])

    share = D // n_img
    r.down[...] = own(r.i_o_down, share)
    r.up[...] = own(r.i_o_up, share)
    both = own(r.i_o_qkv, share)
    r.qkv[...] = both[:, : 3 * D // n_band]
    r.out[...] = both[:, 3 * D // n_band :].T
    vec = r.i_o_vec[...]
    channels = r.i_o_wstat.shape[1]
    r.emb[...] = half(own(r.i_o_emb, channels // n_img))
    mine = lanes(vec, img * share, share)
    for at, name in enumerate(("embed_bias", "ln1_gain", "ln1_bias", "query_bias", "value_bias", "out_bias", "ln2_gain", "ln2_bias", "down_bias")):
        getattr(r, name)[...] = mine[at]
    share = channels // n_img
    r.gn_gain[...] = lanes(vec[8:], img * share, share)[5]
    r.gn_bias[...] = lanes(vec[8:], channels + img * share, share)[5]
    share = FF // n_img
    start = img * share
    line = jnp.sum(jnp.where(iota(vec.shape, 0) == 9 + lax.div(start, D), vec, 0.0), 0, keepdims=True)
    r.up_bias[...] = lanes(jnp.broadcast_to(line, (8, D)), lax.rem(start, D), share)[0]
    cols = channels // n_band
    taps = r.conv.shape[1]
    stats = jnp.concatenate([vec[13:14, 2 * channels :], vec[14:15, :channels], r.i_o_wstat[taps:][:6]], 0)
    stats = lanes(stats, band * cols, cols)
    stand = lanes(r.i_o_wstat[:taps], band * cols, cols)
    grad = half(own(r.i_o_conv, taps)) - stats[0:1] - stand * stats[1:2]
    r.conv[...] = (grad * stats[2:3]).T


def body(
    image,
    conv_weight,
    gn_gain,
    gn_bias,
    embed_weight,
    embed_bias,
    ln1_gain,
    ln1_bias,
    qkv_weight,
    query_bias,
    value_bias,
    out_weight,
    out_bias,
    ln2_gain,
    ln2_bias,
    up_weight,
    up_bias,
    down_weight,
    down_bias,
    text_embed,
    text_len,
    cotangent,
):
    n_img, n_band = lax.axis_size("img"), lax.axis_size("band")
    img, band = lax.axis_index("img"), lax.axis_index("band")
    images, rows = image.shape[:2]
    taps, channels = conv_weight.shape
    img_bits = [("img", k) for k in bits(n_img)]
    one, two, rest = img_bits[:1], img_bits[1:2], img_bits[2:]
    far = [FAR]
    orders = {
        "p_d": (far + one + two, one + two + far, two + one + far),
        "p_u": (far + two + one, one + two + far, two + one + far),
        "p_q": (far + one + two, one + far + two, two + far + one),
    }
    plans = {}
    for name, out in (("p_d", "o_down"), ("p_u", "o_up"), ("p_q", "o_qkv")):
        for k, order in enumerate(orders[name]):
            plans[f"{name}{k}"] = (Plan(n_img, D, 256, FAR, order + rest), out, (0, 256 * k))
    for k in range(3):
        order = (two + one if k == 1 else one + two) + rest + far
        plan = Plan(n_img, taps, channels // 2, None, order, 3)
        plans[f"p_c{k}"] = (plan, "o_conv", (k * plan.rows, 0))
    plans["p_e"] = (Plan(n_img, channels, D // 2, None, two + one + rest + far), "o_emb", (0, 0))
    vec_shape = (16, D)
    arguments = {
        "image": image, "conv_weight": conv_weight, "gn_gain": gn_gain, "gn_bias": gn_bias, "embed_weight": embed_weight,
        "embed_bias": embed_bias, "ln1_gain": ln1_gain, "ln1_bias": ln1_bias, "qkv_weight": qkv_weight, "query_bias": query_bias,
        "value_bias": value_bias, "out_weight": out_weight, "out_bias": out_bias, "ln2_gain": ln2_gain, "ln2_bias": ln2_bias,
        "up_weight": up_weight, "up_bias": up_bias.reshape(1, FF), "down_weight": down_weight, "down_bias": down_bias,
        "text_embed": text_embed, "text_len": text_len, "cotangent": cotangent,
    }
    fetched = ("conv_weight", "embed_weight", "qkv_weight", "cotangent", "text_embed", "out_weight", "up_weight", "down_weight")
    spaces = {name: pl.ANY for name in fetched}
    spaces["text_len"] = pltpu.SMEM
    results = {
        "encoded": (cotangent.shape, HALF),
        "image_grad": (image.shape, FULL),
        "text_grad": (text_embed.shape, FULL),
        "o_down": ((plans["p_d0"][0].rows, D), FULL),
        "o_up": ((plans["p_u0"][0].rows, D), FULL),
        "o_qkv": ((plans["p_q0"][0].rows, D), FULL),
        "o_conv": ((3 * plans["p_c0"][0].rows, channels // 2), FULL),
        "o_emb": ((plans["p_e"][0].rows, D // 2), FULL),
        "o_vec": (vec_shape, FULL),
        "o_wstat": ((taps // n_img + 8, channels), FULL),
    }
    halo = (images, rows + 2, WIDE, channels)
    split = (images, TOK // images, D)
    scratch = {
        "v_" + name: (arguments[name].shape, HALF) for name in fetched
    }
    scratch.update({
        "pixels": (halo, HALF), "views": ((3,) + halo, HALF), "feat": ((TOK, channels), FULL),
        "tap_sum": ((TOK, 128), FULL), "sums": ((n_band, 2 * images, channels), FULL), "sums_back": ((n_band, 2 * images, channels), FULL),
        "zhat": ((TOK, channels), FULL), "active": ((TOK, channels), HALF), "slope": ((TOK, channels), FULL),
        "embedded": (split, HALF), "patches": (split, HALF), "stream": ((TOK, D), FULL), "nhat_one": ((TOK, D), FULL),
        "rstd_one": ((TOK, 1), FULL), "hidden": ((TOK, D), HALF), "qkv": ((TOK, 3 * D), HALF), "probs": ((HEADS, TOK, TOK), HALF),
        "mixed": ((TOK, D), HALF), "nhat_two": ((TOK, D), FULL), "rstd_two": ((TOK, 1), FULL),
        "hidden2": ((TOK, D), HALF), "cot": ((TOK, D), HALF), "final": ((TOK, D), FULL),
        "act": ((4, TOK, D), HALF), "d_pre": ((4, TOK, D), HALF), "up_sum": ((FF // D, 1, D), FULL), "vec": (vec_shape, FULL),
        "d_attn": ((TOK, D), HALF), "d_mixed": ((TOK, D), HALF), "d_qkv": ((TOK, 3 * D), HALF),
        "d_patches": (split, HALF), "d_cells": (split, HALF), "d_feat": ((TOK, channels), HALF), "d_rows": (halo, HALF),
        "d_views": ((3,) + halo, HALF), "mixed_bands": ((4, TOK, 256), HALF), "d_qkv_bands": ((4, TOK, D), HALF), "t_cot": ((D, 2 * TOK), HALF), "t_hidden": ((D, 2 * TOK), HALF), "t_hidden2": ((D, 2 * TOK), HALF), "t_attn": ((D, 2 * TOK), HALF), "slopes": ((4, TOK, D), HALF),
        "r_act": ((2, TOK, D), HALF), "r_d_pre": ((2, TOK, D), HALF),
        "r_d_qkv": ((2, TOK, D), HALF), "r_mixed": ((2, TOK, 256), HALF),
        "r_views": ((3,) + halo, HALF), "r_d_feat": ((TOK, channels), HALF), "r_active": ((TOK, channels), HALF), "r_d_cells": (split, HALF),
    })
    slots = 32
    for name, (plan, _, _) in plans.items():
        for k, shape in enumerate(plan.scratch()):
            scratch[f"{name}_{k}"] = (shape, HALF)
        slots += len(plan.order)
    n_links = 2 + len(img_bits)
    scratch["vec_sum"] = ((n_links,) + vec_shape, FULL)
    scratch["vec_in"] = ((n_links,) + vec_shape, FULL)
    slots += n_links
    sems = {"fetch_sem": 8, "send_sem": slots, "recv_sem": slots}
    names = list(arguments) + list(results) + list(scratch) + list(sems)
    whole = lambda space: pl.BlockSpec(memory_space=space)
    outs = pl.pallas_call(
        functools.partial(layer_kernel, names, plans),
        out_shape=[jax.ShapeDtypeStruct(*v) for v in results.values()],
        in_specs=[whole(spaces.get(name, pltpu.VMEM)) for name in arguments],
        out_specs=[whole(pltpu.VMEM)] * len(results),
        scratch_shapes=[pltpu.VMEM(*v) for v in scratch.values()] + [pltpu.SemaphoreType.DMA((n,)) for n in sems.values()],
        compiler_params=pltpu.CompilerParams(collective_id=0, has_side_effects=True, vmem_limit_bytes=63 * 2**20),
    )(*arguments.values())
    finished = {
        "encoded": (cotangent.shape, HALF),
        "image_grad": (image.shape, FULL),
        "text_grad": (text_embed.shape, FULL),
        "conv": ((channels // n_band, taps // n_img), FULL),
        "gn_gain": ((channels // n_img,), FULL),
        "gn_bias": ((channels // n_img,), FULL),
        "emb": ((channels // n_img, D // n_band), FULL),
        "embed_bias": ((D // n_img,), FULL),
        "ln1_gain": ((D // n_img,), FULL),
        "ln1_bias": ((D // n_img,), FULL),
        "qkv": ((D // n_img, 3 * D // n_band), FULL),
        "query_bias": ((D // n_img,), FULL),
        "value_bias": ((D // n_img,), FULL),
        "out": ((D // n_band, D // n_img), FULL),
        "out_bias": ((D // n_img,), FULL),
        "ln2_gain": ((D // n_img,), FULL),
        "ln2_bias": ((D // n_img,), FULL),
        "up": ((D // n_img, FF // n_band), FULL),
        "up_bias": ((FF // n_img,), FULL),
        "down": ((D // n_img, FF // n_band), FULL),
        "down_bias": ((D // n_img,), FULL),
    }
    names = ["i_" + name for name in results] + list(finished)
    outs = pl.pallas_call(
        functools.partial(finish_kernel, names),
        out_shape=[jax.ShapeDtypeStruct(*v) for v in finished.values()],
        in_specs=[whole(pltpu.VMEM)] * len(results),
        out_specs=[whole(pltpu.VMEM)] * len(finished),
    )(*outs)
    res = dict(zip(finished, outs))
    res["conv"], res["down"] = res["conv"].T, res["down"].T
    return tuple(res.values())


def solution(mesh):
    in_specs = (
        P("img", "band", None, None),
        P(),
        P(),
        P(),
        P(),
        P(),
        P(),
        P(),
        P(),
        P(),
        P(),
        P(),
        P(),
        P(),
        P(),
        P(),
        P(),
        P(),
        P(),
        P(("img", "band"), None, None),
        P(("img", "band")),
        P(("img", "band"), None, None),
    )
    out_specs = (
        P(("img", "band"), None, None),
        P("img", "band", None, None),
        P(("img", "band"), None, None),
        P("img", "band"),
        P("img"),
        P("img"),
        P("img", "band"),
        P("img"),
        P("img"),
        P("img"),
        P("img", "band"),
        P("img"),
        P("img"),
        P("band", "img"),
        P("img"),
        P("img"),
        P("img"),
        P("img", "band"),
        P("img"),
        P("band", "img"),
        P("img"),
    )
    return jax.shard_map(body, mesh=mesh, in_specs=in_specs, out_specs=out_specs, check_vma=False)
```

time: 186 us -> 116 us (0.62)
  Pallas kernels: 160 us -> 112 us
  local copies, waits for them, and re-layouts: 22.4 us -> 3.36 us
    pallas_call x1, Pallas kernels: 160 us -> 107 us  [body(): pl.pallas_call(functools.partial(layer_kernel, names, plans), out_shape=[...]
    unnamed x11 -> x2, local copies, waits for them, and re-layouts: 12.2 us -> 3.36 us
    dynamic_slice x9 -> x0, local copies, waits for them, and re-layouts: 6.24 us -> none  [the longest x8 4.75 us: own(): lax.dynamic_slice_in_dim(v, lax.rem(img, v.shape[axis] // size) * size, s...]
    pallas_call x0 -> x1, Pallas kernels: none -> 4.43 us  [body(): pl.pallas_call(functools.partial(finish_kernel, names), out_shape=[jax.Sh...]
    slice x3 -> x0, local copies, waits for them, and re-layouts: 2.77 us -> none  [the longest x2 2.03 us: own_vec(): return own(vec[at, lo:lo + total], total)]
where the time goes in v3:
time: 116 us
  Pallas kernels  112 us (97%)
  local copies, waits for them, and re-layouts  3.36 us (3%)
  between operations  1.32 us (1%)
    pallas_call x1, Pallas kernels, body(): pl.pallas_call(functools.partial(layer_kernel, names, plans), out_shape=[...  107 us
    pallas_call x1, Pallas kernels, body(): pl.pallas_call(functools.partial(finish_kernel, names), out_shape=[jax.Sh...  4.43 us
    unnamed x2, local copies, waits for them, and re-layouts  3.36 us

profile of v3, /device:TPU:0, one launch (start us, length us, event | category | flops | bytes accessed | tf_op | source)
XLA Modules:
  0.0 116.3 jit_solution(2017857951182368564)
XLA Ops:
  1.3 1.6 %copy.43.refs_0_ = bf16[4,4,14,256]{3,2,1,0:T(8,128)(2,1)} copy(bf16[4,4,14,256]{3,1,2,0:T(4,128)(2,1)} %param.22) | data formatting | bytes 229376 | tf_op args[0]
  2.9 107.2 %shard_map.373 = (bf16[1,228,768]{2,1,0:T(8,128)(2,1)}, f32[4,4,14,256]{3,2,1,0:T(8,128)}, f32[1,32,768]{2,1,0:T(8,128)}, f32[96,768]{1,0:T(8,128)}, f32[96,768]...) custom-call(bf16[4,4,14,256]{3,2,1,0:T(8,128)(2,1)} %copy.43.refs_0_, ...), custom_call_target="tpu_custom_call" | custom-call | tf_op jit(solution)/shard_map/pallas_call | solution.py:796
  110.0 4.4 %shard_map.374 = (bf16[1,228,768]{2,1,0:T(8,128)(2,1)}, f32[4,4,14,256]{3,2,1,0:T(8,128)}, f32[1,32,768]{2,1,0:T(8,128)}, f32[64,288]{1,0:T(8,128)}, f32[32]{0:T...) custom-call(bf16[1,228,768]{2,1,0:T(8,128)(2,1)} %get-tuple-element., ...), custom_call_target="tpu_custom_call" | custom-call | tf_op jit(solution)/shard_map/pallas_call | solution.py:828
  114.5 1.8 %copy.44 = f32[4,4,14,256]{3,1,2,0:T(4,128)} copy(f32[4,4,14,256]{3,2,1,0:T(8,128)} %get-tuple-element.84) | data formatting | bytes 458752

commit v4 on v3

--- a/solution.py
+++ b/solution.py
@@ -48,6 +48,12 @@
     return [1 << k for k in range(count.bit_length() - 1)]
 
 
+def route(letters, n_img):
+    near = [("img", k) for k in bits(n_img)]
+    routes = {"c": [CORE], "y": [FAR], "Y": [FAR], "x": near[:1], "z": near[1:2], "w": near[2:]}
+    return sum((routes[letter] for letter in letters), [])
+
+
 class Plan:
     def __init__(self, n_img, rows, width, lead, order, parts=1):
         self.width = width
@@ -55,8 +61,7 @@
         self.rows = (rows >> len(split)) // parts
         self.first = ([lead] if lead else []) + split
         rest = [("img", k) for k in bits(n_img) if ("img", k) not in split]
-        ordered = [lab for lab in order if lab in self.first]
-        self.order = ordered + rest + [lab for lab in order if lab not in self.first and lab[0] == "band"]
+        self.order = [lab for lab in order if lab not in rest] + rest
         self.shapes = []
         labels = list(self.first)
         for lab in self.order:
@@ -180,14 +185,97 @@
     return left, values, right
 
 
-DOWN, UP, QKV, TAIL = ("p_d0", "p_d1", "p_d2"), ("p_u0", "p_u1", "p_u2"), ("p_q0", "p_q1", "p_q2"), ("p_c0", "p_c1", "p_c2", "p_e")
+DOWN, UP, QKV = ("p_d0", "p_d1", "p_d2"), ("p_u0", "p_u1", "p_u2"), ("p_q0", "p_q1", "p_q2")
+ORDERS = {
+    "p_d0": "xzwy",
+    "p_d1": "yzxw",
+    "p_d2": "zxyw",
+    "p_u0": "yxzw",
+    "p_u1": "xyzw",
+    "p_u2": "wyxz",
+    "p_q0": "yxzw",
+    "p_q1": "xzyw",
+    "p_q2": "yxzw",
+    "p_c0": "xzYw",
+    "p_c1": "xwzY",
+    "p_c2": "xzwY",
+    "p_e": "zxwY",
+    "vec": "zwycx",
+}
 POLLS = {
-    "back1": DOWN,
-    "cells": ("qkv",) + UP + ("+p_q1", "+p_q2"),
-    "sums": ("p_d1",),
-    "edges": ("p_d0", "p_d2", "p_u1", "+p_q0"),
-    "grad": ("p_u0", "p_u2"),
-    "end": DOWN + ("p_q1", "p_q2", "p_q0") + TAIL + UP + DOWN + ("vec",) + QKV + TAIL + UP + ("vec",) + QKV + ("vec",) + TAIL + QKV + ("vec",) + TAIL + ("vec",),
+    "back1": (
+        "p_d0",
+        "p_d1",
+        "p_d2",
+    ),
+    "cells": (
+        "qkv",
+        "+p_q1",
+        "p_u1",
+        "p_u0",
+    ),
+    "sums": (
+        "p_d2",
+        "p_d0",
+    ),
+    "edges": (
+        "+p_q2",
+        "+p_q0",
+        "p_u1",
+        "p_u2",
+        "p_d1",
+        "p_d2",
+    ),
+    "grad": (
+        "p_q1",
+        "vec",
+        "p_d0",
+    ),
+    "end": (
+        "p_u1",
+        "p_u0",
+        "p_d2",
+        "p_d1",
+        "p_q2",
+        "p_q1",
+        "p_c0",
+        "vec",
+        "p_c1",
+        "p_e",
+        "p_c2",
+        "p_u1",
+        "p_u0",
+        "p_q0",
+        "p_c0",
+        "p_d1",
+        "p_q2",
+        "p_e",
+        "p_c2",
+        "p_c1",
+        "p_u2",
+        "p_u0",
+        "p_d0",
+        "p_q2",
+        "p_q0",
+        "p_e",
+        "p_q1",
+        "p_c2",
+        "p_c1",
+        "p_u2",
+        "vec",
+        "p_c0",
+        "p_q2",
+        "p_e",
+        "vec",
+        "p_c2",
+        "p_q0",
+        "p_c1",
+        "p_u2",
+        "p_q1",
+        "vec",
+        "p_c0",
+        "p_q0",
+    ),
 }
 
 
@@ -195,7 +283,7 @@
     r = types.SimpleNamespace(**dict(zip(names, refs)))
     img, band = lax.axis_index("img"), lax.axis_index("band")
     n_img, n_band = lax.axis_size("img"), lax.axis_size("band")
-    images, rows = r.image.shape[:2]
+    images, _, rows = r.image.shape[:3]
     channels = r.conv_weight.shape[1]
     core = my_bit(CORE)
     others = [lax.rem(band + d, n_band) for d in range(n_band)]
@@ -206,7 +294,7 @@
         copy = pltpu.make_async_copy(getattr(r, name), getattr(r, "v_" + name), r.fetch_sem.at[at])
         fetches[name] = Once(copy)
 
-    for at, name in enumerate(("conv_weight", "embed_weight", "qkv_weight", "cotangent", "text_embed", "out_weight", "up_weight", "down_weight")):
+    for at, name in enumerate(("cotangent", "conv_weight", "embed_weight", "qkv_weight", "text_embed", "out_weight", "up_weight", "down_weight")):
         fetch(name, at)
 
     links = [CORE, FAR] + [("img", k) for k in bits(n_img)]
@@ -215,7 +303,6 @@
         pl.semaphore_signal(barrier, inc=1, device_id=(img, others[d]), device_id_type=MESH_ID)
     for label in links[2:]:
         pl.semaphore_signal(barrier, inc=1, device_id=partner(label), device_id_type=MESH_ID)
-    pl.semaphore_wait(barrier, n_band - 1 + len(links) - 2)
 
     pending = []
 
@@ -312,10 +399,9 @@
                 piece.start()
 
     r.pixels[:, 1 : rows + 1, GRID:, :] = jnp.zeros((images, rows, WIDE - GRID, channels), HALF)
-    at_row = iota((images, rows, GRID, channels), 1) + band * rows
-    r.pixels[:, 1 : rows + 1, :GRID, :] = jnp.where(at_row < GRID, r.image[...].astype(FULL), 0.0).astype(HALF)
-    copies = edge_rows(r.pixels, 0)
-
+    for k in range(rows):
+        line = r.image[:, :, k, :].astype(FULL)
+        r.pixels[:, k + 1, :GRID, :] = jnp.where(band * rows + k < GRID, line, 0.0).astype(HALF)
     fetches["cotangent"].wait()
     seq = r.cotangent.shape[1]
 
@@ -327,6 +413,9 @@
     r.cot[...] = dot(spread, r.v_cotangent[0]).astype(HALF)
 
     r.t_cot[:, :TOK] = r.cot[...].T
+    pl.semaphore_wait(barrier, n_band - 1 + len(links) - 2)
+    copies = edge_rows(r.pixels, 0)
+
     swap_left("down", 0, r.t_cot)
 
     fetches["conv_weight"].wait()
@@ -351,6 +440,7 @@
     pixels = edges_in(r.pixels, copies)
     for e, values in enumerate(shifted(pixels)):
         r.views[e] = values.astype(HALF)
+    swap("conv", 12, r.views, r.r_views)
 
     def window(views, a, e):
         return views[e, :, a : a + rows].reshape(TOK, channels)
@@ -388,6 +478,7 @@
     stem, slope = gelu_parts(zhat * row(r.gn_gain) + row(r.gn_bias))
     r.active[...] = jnp.where(live, stem, 0.0).astype(HALF)
     r.slope[...] = jnp.where(live, slope, 0.0)
+    swap("emb", 14, r.active, r.r_active)
     fetches["embed_weight"].wait()
     embedded = dot(r.active[...], r.v_embed_weight[...]) + row(r.embed_bias)
     r.embedded[...] = embedded.astype(HALF).reshape(images, cells, D)
@@ -425,12 +516,12 @@
     zero = jnp.zeros((TOK, 128), HALF)
 
     def pair_of(ref, k, p):
-        return ref[:, pl.ds(pl.multiple_of(k * D + p * 128, 128), 128)]
+        return ref[:, k * D + p * 128 : k * D + (p + 1) * 128]
 
     def only(values, h):
         return jnp.where(first, values, zero) if h == 0 else jnp.where(first, zero, values)
 
-    def attend(p, carry):
+    def attend(p):
         query, key, value = (pair_of(r.qkv, k, p) for k in range(3))
         sides = []
         for h in range(2):
@@ -440,10 +531,10 @@
             probs = probs.astype(HALF)
             r.probs[2 * p + h] = probs
             sides.append(dot(probs, value))
-        r.mixed[:, pl.ds(pl.multiple_of(p * 128, 128), 128)] = jnp.where(first, *sides).astype(HALF)
-        return carry
-
-    lax.fori_loop(0, HEADS // 2, attend, 0)
+        r.mixed[:, p * 128 : (p + 1) * 128] = jnp.where(first, *sides).astype(HALF)
+
+    for p in range(HEADS // 2):
+        attend(p)
     for k in range(4):
         width = D // 4
         r.mixed_bands[k] = jnp.concatenate([jnp.zeros((TOK, 256 - width), HALF), r.mixed[:, k * width : (k + 1) * width]], 1)
@@ -459,14 +550,11 @@
     r.t_hidden2[:, :TOK] = r.hidden2[...].T
     swap_left("up", 3, r.t_hidden2)
 
-    def feed(k, carry):
-        wide = pl.ds(pl.multiple_of(k * D, 128), D)
+    for k in range(FF // D):
+        wide = slice(k * D, (k + 1) * D)
         act, slope = gelu_parts(dot(r.hidden2[...], r.v_up_weight[:, wide]) + r.up_bias[:, wide])
         r.act[k] = act.astype(HALF)
         r.slopes[k] = slope.astype(HALF)
-        return carry
-
-    lax.fori_loop(0, FF // D, feed, 0)
     swap_bands("down", 1, r.act, r.r_act)
     fetches["down_weight"].wait()
     final = r.final[...]
@@ -476,14 +564,11 @@
     arrived("down")
     unit(down, [(r.t_cot, r.act, r.r_act, 0)])
 
-    def feed_back(k, carry):
-        wide = pl.ds(pl.multiple_of(k * D, 128), D)
+    for k in range(FF // D):
+        wide = slice(k * D, (k + 1) * D)
         d_pre = dot_nt(r.cot[...], r.v_down_weight[wide, :]) * r.slopes[k].astype(FULL)
         r.d_pre[k] = d_pre.astype(HALF)
         r.up_sum[k] = column_sum(r.d_pre[k].astype(FULL))
-        return carry
-
-    lax.fori_loop(0, FF // D, feed_back, 0)
     swap_bands("up", 4, r.d_pre, r.r_d_pre)
     grad = 0.0
     for k in range(FF // D):
@@ -511,7 +596,7 @@
 
     arrived("up")
     unit(up, [(r.t_hidden2, r.d_pre, r.r_d_pre, 0)])
-    def attend_back(p, carry):
+    def attend_back(p):
         query, key, value = (pair_of(r.qkv, k, p) for k in range(3))
         d_mixed = pair_of(r.d_mixed, 0, p)
         sides = [[], [], []]
@@ -525,12 +610,11 @@
             sides[1].append(dot_tn(d_scores, query))
             sides[2].append(dot_tn(probs, d_mixed))
         for k in range(3):
-            r.d_qkv[:, pl.ds(pl.multiple_of(k * D + p * 128, 128), 128)] = jnp.where(first, *sides[k]).astype(HALF)
-        return carry
-
-    for part in range(3):
-        lax.fori_loop(HEADS // 6 * part, HEADS // 6 * (part + 1), attend_back, 0)
-        poll(f"back{part}")
+            r.d_qkv[:, k * D + p * 128 : k * D + (p + 1) * 128] = jnp.where(first, *sides[k]).astype(HALF)
+
+    for p in range(HEADS // 2):
+        attend_back(p)
+        poll(f"back{p}")
     for k in range(4):
         width = 3 * D // 4
         r.d_qkv_bands[k] = jnp.concatenate([r.d_qkv[:, k * width : (k + 1) * width], jnp.zeros((TOK, D - width), HALF)], 1)
@@ -549,6 +633,7 @@
         arrived("out")
         unit(qkv, [(r.t_hidden, r.d_qkv_bands, r.r_d_qkv, 0), (r.t_attn, r.mixed_bands, r.r_mixed, 2)], False)
     to_owners(r.d_patches, r.d_cells, 8, "cells")
+    swap("emb", 15, r.d_cells, r.r_d_cells)
     d_cells = r.d_cells[...].reshape(TOK, D)
     put(0, column_sum(d_cells.astype(FULL)))
     d_active = dot_nt(d_cells, r.v_embed_weight[...]).astype(HALF).astype(FULL)
@@ -564,12 +649,15 @@
     r.d_feat[...] = d_feat
     r.d_rows[:, 1 : rows + 1] = d_feat.reshape(images, rows, WIDE, channels)
     copies = edge_rows(r.d_rows, 14)
+    swap("conv", 13, r.d_feat, r.r_d_feat)
     d_feat = d_feat.astype(FULL)
     put(13, column_sum(r.tap_sum[:, :1] * d_feat) * (1.0 / taps), 2 * channels)
     put(14, column_sum(r.feat[...] * d_feat) * (1.0 / taps))
 
+    vec_links = route(ORDERS["vec"], n_img)
+
     def vec_start(stage):
-        return send(r.vec if stage == 0 else r.vec_sum.at[stage - 1], r.vec_in.at[stage], slot + stage, partner(links[stage]))
+        return send(r.vec if stage == 0 else r.vec_sum.at[stage - 1], r.vec_in.at[stage], slot + stage, partner(vec_links[stage]))
 
     vec_state = [r.vec[...], 0, vec_start(0)]
 
@@ -596,10 +684,6 @@
     r.image_grad[...] = grad[:, :, :GRID]
 
     poll("grad")
-    swap("conv", 12, r.views, r.r_views)
-    swap("conv", 13, r.d_feat, r.r_d_feat)
-    swap("emb", 14, r.active, r.r_active)
-    swap("emb", 15, r.d_cells, r.r_d_cells)
 
     def columns(values, width):
         total = values.shape[1]
@@ -646,8 +730,10 @@
     img, band = lax.axis_index("img"), lax.axis_index("band")
     n_img, n_band = lax.axis_size("img"), lax.axis_size("band")
     far = my_bit(FAR)
-    for name in ("encoded", "image_grad", "text_grad"):
-        getattr(r, name)[...] = getattr(r, "i_" + name)[...]
+    r.encoded[...] = r.i_encoded[...]
+    r.text_grad[...] = r.i_text_grad[...]
+    for k in range(r.image_grad.shape[2]):
+        r.image_grad[:, :, k, :] = r.i_image_grad[:, k]
 
     def own(ref, rows):
         if ref.shape[0] == rows:
@@ -721,31 +807,29 @@
     images, rows = image.shape[:2]
     taps, channels = conv_weight.shape
     img_bits = [("img", k) for k in bits(n_img)]
-    one, two, rest = img_bits[:1], img_bits[1:2], img_bits[2:]
-    far = [FAR]
-    orders = {
-        "p_d": (far + one + two, one + two + far, two + one + far),
-        "p_u": (far + two + one, one + two + far, two + one + far),
-        "p_q": (far + one + two, one + far + two, two + far + one),
-    }
     plans = {}
-    for name, out in (("p_d", "o_down"), ("p_u", "o_up"), ("p_q", "o_qkv")):
-        for k, order in enumerate(orders[name]):
-            plans[f"{name}{k}"] = (Plan(n_img, D, 256, FAR, order + rest), out, (0, 256 * k))
-    for k in range(3):
-        order = (two + one if k == 1 else one + two) + rest + far
-        plan = Plan(n_img, taps, channels // 2, None, order, 3)
-        plans[f"p_c{k}"] = (plan, "o_conv", (k * plan.rows, 0))
-    plans["p_e"] = (Plan(n_img, channels, D // 2, None, two + one + rest + far), "o_emb", (0, 0))
+    for name, order in ORDERS.items():
+        if name == "vec":
+            continue
+        order = route(order, n_img)
+        k = int(name[3:] or 0)
+        if name in DOWN + UP + QKV:
+            out = {"d": "o_down", "u": "o_up", "q": "o_qkv"}[name[2]]
+            plans[name] = (Plan(n_img, D, 256, FAR, order), out, (0, 256 * k))
+        elif name == "p_e":
+            plans[name] = (Plan(n_img, channels, D // 2, None, order), "o_emb", (0, 0))
+        else:
+            plan = Plan(n_img, taps, channels // 2, None, order, 3)
+            plans[name] = (plan, "o_conv", (k * plan.rows, 0))
     vec_shape = (16, D)
     arguments = {
-        "image": image, "conv_weight": conv_weight, "gn_gain": gn_gain, "gn_bias": gn_bias, "embed_weight": embed_weight,
+        "image": image.transpose(0, 2, 1, 3), "conv_weight": conv_weight, "gn_gain": gn_gain, "gn_bias": gn_bias, "embed_weight": embed_weight,
         "embed_bias": embed_bias, "ln1_gain": ln1_gain, "ln1_bias": ln1_bias, "qkv_weight": qkv_weight, "query_bias": query_bias,
         "value_bias": value_bias, "out_weight": out_weight, "out_bias": out_bias, "ln2_gain": ln2_gain, "ln2_bias": ln2_bias,
         "up_weight": up_weight, "up_bias": up_bias.reshape(1, FF), "down_weight": down_weight, "down_bias": down_bias,
         "text_embed": text_embed, "text_len": text_len, "cotangent": cotangent,
     }
-    fetched = ("conv_weight", "embed_weight", "qkv_weight", "cotangent", "text_embed", "out_weight", "up_weight", "down_weight")
+    fetched = ("cotangent", "conv_weight", "embed_weight", "qkv_weight", "text_embed", "out_weight", "up_weight", "down_weight")
     spaces = {name: pl.ANY for name in fetched}
     spaces["text_len"] = pltpu.SMEM
     results = {
@@ -803,7 +887,7 @@
     )(*arguments.values())
     finished = {
         "encoded": (cotangent.shape, HALF),
-        "image_grad": (image.shape, FULL),
+        "image_grad": (arguments["image"].shape, FULL),
         "text_grad": (text_embed.shape, FULL),
         "conv": ((channels // n_band, taps // n_img), FULL),
         "gn_gain": ((channels // n_img,), FULL),
@@ -833,6 +917,7 @@
     )(*outs)
     res = dict(zip(finished, outs))
     res["conv"], res["down"] = res["conv"].T, res["down"].T
+    res["image_grad"] = res["image_grad"].transpose(0, 2, 1, 3)
     return tuple(res.values())
 
 

time: 116 us -> 101 us (0.87)
  Pallas kernels: 112 us -> 99.7 us
  local copies, waits for them, and re-layouts: 3.36 us -> 0 us
    pallas_call x1, Pallas kernels: 107 us -> 95.3 us  [body(): pl.pallas_call(functools.partial(layer_kernel, names, plans), out_shape=[...]
    unnamed x2 -> x0, local copies, waits for them, and re-layouts: 3.36 us -> none
where the time goes in v4:
time: 101 us
  Pallas kernels  99.7 us (99%)
  between operations  1.5 us (1%)
    pallas_call x1, Pallas kernels, body(): pl.pallas_call(functools.partial(layer_kernel, names, plans), out_shape=[...  95.3 us
    pallas_call x1, Pallas kernels, body(): pl.pallas_call(functools.partial(finish_kernel, names), out_shape=[jax.Sh...  4.45 us

profile of v4, /device:TPU:0, one launch (start us, length us, event | category | flops | bytes accessed | tf_op | source)
XLA Modules:
  0.0 101.2 jit_solution(6280537464368057395)
XLA Ops:
  1.3 95.3 %shard_map.373 = (bf16[1,228,768]{2,1,0:T(8,128)(2,1)}, f32[4,4,14,256]{3,2,1,0:T(8,128)}, f32[1,32,768]{2,1,0:T(8,128)}, f32[96,768]{1,0:T(8,128)}, f32[96,768]...) custom-call(bf16[4,14,4,256]{3,2,1,0:T(4,128)(2,1)} %bitcast.5, ...), custom_call_target="tpu_custom_call" | custom-call | tf_op jit(solution)/shard_map/pallas_call | solution.py:880
  96.6 4.5 %shard_map.374 = (bf16[1,228,768]{2,1,0:T(8,128)(2,1)}, f32[4,14,4,256]{3,2,1,0:T(4,128)}, f32[1,32,768]{2,1,0:T(8,128)}, f32[64,288]{1,0:T(8,128)}, f32[32]{0:T...) custom-call(bf16[1,228,768]{2,1,0:T(8,128)(2,1)} %get-tuple-element., ...), custom_call_target="tpu_custom_call" | custom-call | tf_op jit(solution)/shard_map/pallas_call | solution.py:912

commit v5 on v4

--- a/solution.py
+++ b/solution.py
@@ -185,7 +185,7 @@
     return left, values, right
 
 
-DOWN, UP, QKV = ("p_d0", "p_d1", "p_d2"), ("p_u0", "p_u1", "p_u2"), ("p_q0", "p_q1", "p_q2")
+DOWN, UP, QKV = (tuple(f"p_{unit}{k}" for k in range(3)) for unit in "duq")
 ORDERS = {
     "p_d0": "xzwy",
     "p_d1": "yzxw",
@@ -440,7 +440,6 @@
     pixels = edges_in(r.pixels, copies)
     for e, values in enumerate(shifted(pixels)):
         r.views[e] = values.astype(HALF)
-    swap("conv", 12, r.views, r.r_views)
 
     def window(views, a, e):
         return views[e, :, a : a + rows].reshape(TOK, channels)
@@ -478,11 +477,12 @@
     stem, slope = gelu_parts(zhat * row(r.gn_gain) + row(r.gn_bias))
     r.active[...] = jnp.where(live, stem, 0.0).astype(HALF)
     r.slope[...] = jnp.where(live, slope, 0.0)
-    swap("emb", 14, r.active, r.r_active)
     fetches["embed_weight"].wait()
     embedded = dot(r.active[...], r.v_embed_weight[...]) + row(r.embed_bias)
     r.embedded[...] = embedded.astype(HALF).reshape(images, cells, D)
     to_owners(r.embedded, r.patches, 5)
+    swap("conv", 12, r.views, r.r_views)
+    swap("emb", 14, r.active, r.r_active)
     def norm(values):
         mean = jnp.mean(values, -1, keepdims=True)
         cent = values - mean
@@ -560,9 +560,9 @@
     final = r.final[...]
     for k in range(FF // D):
         final = final + dot(r.act[k], r.v_down_weight[k * D : (k + 1) * D])
-    r.encoded[0] = dot(gather, final.astype(HALF)).astype(HALF)
     arrived("down")
     unit(down, [(r.t_cot, r.act, r.r_act, 0)])
+    r.encoded[0] = dot(gather, final.astype(HALF)).astype(HALF)
 
     for k in range(FF // D):
         wide = slice(k * D, (k + 1) * D)

time: 101 us -> 100 us (0.990)
  no operation moved by 1% of the time
where the time goes in v5:
time: 100 us
  Pallas kernels  98.8 us (99%)
  between operations  1.5 us (2%)
    pallas_call x1, Pallas kernels, body(): pl.pallas_call(functools.partial(layer_kernel, names, plans), out_shape=[...  94.3 us
    pallas_call x1, Pallas kernels, body(): pl.pallas_call(functools.partial(finish_kernel, names), out_shape=[jax.Sh...  4.45 us

profile of v5, /device:TPU:0, one launch (start us, length us, event | category | flops | bytes accessed | tf_op | source)
XLA Modules:
  0.0 100.3 jit_solution(3176273648695941726)
XLA Ops:
  1.3 94.3 %shard_map.373 = (bf16[1,228,768]{2,1,0:T(8,128)(2,1)}, f32[4,4,14,256]{3,2,1,0:T(8,128)}, f32[1,32,768]{2,1,0:T(8,128)}, f32[96,768]{1,0:T(8,128)}, f32[96,768]...) custom-call(bf16[4,14,4,256]{3,2,1,0:T(4,128)(2,1)} %bitcast.5, ...), custom_call_target="tpu_custom_call" | custom-call | tf_op jit(solution)/shard_map/pallas_call | solution.py:880
  95.6 4.5 %shard_map.374 = (bf16[1,228,768]{2,1,0:T(8,128)(2,1)}, f32[4,14,4,256]{3,2,1,0:T(4,128)}, f32[1,32,768]{2,1,0:T(8,128)}, f32[64,288]{1,0:T(8,128)}, f32[32]{0:T...) custom-call(bf16[1,228,768]{2,1,0:T(8,128)(2,1)} %get-tuple-element., ...), custom_call_target="tpu_custom_call" | custom-call | tf_op jit(solution)/shard_map/pallas_call | solution.py:912

commit v6 on v5

--- a/solution.py
+++ b/solution.py
@@ -501,8 +501,6 @@
     r.nhat_one[...] = nhat
     r.rstd_one[...] = rstd_one
     r.hidden[...] = (nhat * row(r.ln1_gain) + row(r.ln1_bias)).astype(HALF)
-    r.t_hidden[:, :TOK] = r.hidden[...].T
-    swap_left("qkv", 6, r.t_hidden)
     fetches["qkv_weight"].wait()
     for k, bias in enumerate((r.query_bias, None, r.value_bias)):
         values = dot(r.hidden[...], r.v_qkv_weight[:, k * D : (k + 1) * D])
@@ -535,10 +533,6 @@
 
     for p in range(HEADS // 2):
         attend(p)
-    for k in range(4):
-        width = D // 4
-        r.mixed_bands[k] = jnp.concatenate([jnp.zeros((TOK, 256 - width), HALF), r.mixed[:, k * width : (k + 1) * width]], 1)
-    swap_bands("out", 10, r.mixed_bands, r.r_mixed)
     fetches["out_weight"].wait()
     mid = r.stream[...] + dot(r.mixed[...], r.v_out_weight[...]) + row(r.out_bias)
     r.final[...] = mid + row(r.down_bias)
@@ -547,8 +541,6 @@
     r.rstd_two[...] = rstd_two
     r.hidden2[...] = (nhat * row(r.ln2_gain) + row(r.ln2_bias)).astype(HALF)
     fetches["up_weight"].wait()
-    r.t_hidden2[:, :TOK] = r.hidden2[...].T
-    swap_left("up", 3, r.t_hidden2)
 
     for k in range(FF // D):
         wide = slice(k * D, (k + 1) * D)
@@ -562,6 +554,8 @@
         final = final + dot(r.act[k], r.v_down_weight[k * D : (k + 1) * D])
     arrived("down")
     unit(down, [(r.t_cot, r.act, r.r_act, 0)])
+    r.t_hidden2[:, :TOK] = r.hidden2[...].T
+    swap_left("up", 3, r.t_hidden2)
     r.encoded[0] = dot(gather, final.astype(HALF)).astype(HALF)
 
     for k in range(FF // D):
@@ -596,6 +590,12 @@
 
     arrived("up")
     unit(up, [(r.t_hidden2, r.d_pre, r.r_d_pre, 0)])
+    r.t_hidden[:, :TOK] = r.hidden[...].T
+    swap_left("qkv", 6, r.t_hidden)
+    for k in range(4):
+        width = D // 4
+        r.mixed_bands[k] = jnp.concatenate([jnp.zeros((TOK, 256 - width), HALF), r.mixed[:, k * width : (k + 1) * width]], 1)
+    swap_bands("out", 10, r.mixed_bands, r.r_mixed)
     def attend_back(p):
         query, key, value = (pair_of(r.qkv, k, p) for k in range(3))
         d_mixed = pair_of(r.d_mixed, 0, p)

time: 100 us -> 100 us (level)
  no operation moved by 1% of the time
where the time goes in v6:
time: 100 us
  Pallas kernels  98.5 us (98%)
  between operations  1.5 us (2%)
    pallas_call x1, Pallas kernels, body(): pl.pallas_call(functools.partial(layer_kernel, names, plans), out_shape=[...  94 us
    pallas_call x1, Pallas kernels, body(): pl.pallas_call(functools.partial(finish_kernel, names), out_shape=[jax.Sh...  4.45 us

profile of v6, /device:TPU:0, one launch (start us, length us, event | category | flops | bytes accessed | tf_op | source)
XLA Modules:
  0.0 100.0 jit_solution(53789993952150963)
XLA Ops:
  1.3 94.0 %shard_map.373 = (bf16[1,228,768]{2,1,0:T(8,128)(2,1)}, f32[4,4,14,256]{3,2,1,0:T(8,128)}, f32[1,32,768]{2,1,0:T(8,128)}, f32[96,768]{1,0:T(8,128)}, f32[96,768]...) custom-call(bf16[4,14,4,256]{3,2,1,0:T(4,128)(2,1)} %bitcast.5, ...), custom_call_target="tpu_custom_call" | custom-call | tf_op jit(solution)/shard_map/pallas_call | solution.py:880
  95.3 4.5 %shard_map.374 = (bf16[1,228,768]{2,1,0:T(8,128)(2,1)}, f32[4,14,4,256]{3,2,1,0:T(4,128)}, f32[1,32,768]{2,1,0:T(8,128)}, f32[64,288]{1,0:T(8,128)}, f32[32]{0:T...) custom-call(bf16[1,228,768]{2,1,0:T(8,128)(2,1)} %get-tuple-element., ...), custom_call_target="tpu_custom_call" | custom-call | tf_op jit(solution)/shard_map/pallas_call | solution.py:912
